TPU v7x, 512 devices: a whole 4x8x8 slice. The times are simulated.
512 devices in a mesh: seq: 64 (over x, y_hi, z), tensor: 8 (over y_lo, core).
Axes of the slice: x: 4, y: 8 (y_hi: 2, y_lo: 4; y = y_hi * 4 + y_lo), z: 8, core: 2. Of those that a mesh axis runs over, the one named last changes fastest.
Arguments:
- queries: bfloat16 [16384, 8192], P('seq', 'tensor'), may hold values from -6 to 6
- features: bfloat16 [6144, 4096], P('seq'), may hold values from -6 to 6
- w_key: bfloat16 [4096, 1024], P(None, 'tensor'), may hold values from -0.09375 to 0.09375
- w_value: bfloat16 [4096, 1024], P(None, 'tensor'), may hold values from -0.5 to 0.5
- q_gain: float32 [128], replicated, may hold values from 0.1 to 1.9
- k_gain: float32 [128], replicated, may hold values from 0.1 to 1.9
- slot_image: int32 [64], replicated, may hold values from 0 to 63, as said below
- image_tiles: int32 [64], replicated, may hold values from 1 to 4
- image_range: int32 [256, 2], P('seq'), may hold values from 0 to 64, as said below
- d_out: bfloat16 [16384, 8192], P('seq', 'tensor'), may hold values from -6 to 6
Outputs:
- attended: bfloat16 [16384, 8192], P('seq', 'tensor')
- grad_queries: bfloat16 [16384, 8192], P('seq', 'tensor')
- grad_features: bfloat16 [6144, 4096], P('seq', 'tensor')
Inputs may be any that keep to these rules, and one draw needn't show every extreme that they name: `slot_image`: a permutation; each image id is encoded in a slot of its own aligned group of 4 slots. `image_range`: for a block among the tokens of seq index s: max(0, s - 2) <= first <= last <= s + 1; first == last means the block attends no image.
All inputs are finite; a program needn't handle non-finite values.
Results may differ from a plain program's by a relative error of at most 0.019.
Values may be sent and summed in bfloat16 or wider, within the bound.
A program may use at most 64 MiB of HBM per device.

v0:
```python
import jax
import jax.numpy as jnp
from jax import lax
from jax.sharding import PartitionSpec as P

TILE_ROWS = 24
GROUP = 4
LOOKBACK = 3


def from_behind(array, axis, by):
    devices = lax.axis_size(axis)
    pairs = [(i, i + by) for i in range(devices) if 0 <= i + by < devices]
    return lax.ppermute(array, axis, pairs)


def rms_scale(values, gain_vector):
    inverse = lax.rsqrt(jnp.mean(values * values, axis=-1, keepdims=True) + 1e-05)
    return (values * inverse * gain_vector, inverse)


def rms_back(values, inverse, gain_vector, upstream):
    scaled = gain_vector * upstream
    return inverse * scaled - values * inverse**3 * jnp.mean(
        scaled * values, axis=-1, keepdims=True
    )


def local(
    queries, features, w_key, w_value, q_gain, k_gain, slot_image, image_tiles, image_range, d_out
):
    seq_count = lax.axis_size("seq")
    seq_index = lax.axis_index("seq")
    head_size = q_gain.shape[0]
    tok_count = queries.shape[0]
    row_count = features.shape[0]
    kv_local = w_key.shape[1] // head_size
    group_size = queries.shape[1] // (kv_local * head_size)
    score_scale = head_size ** (-0.5)
    lowest = 1 - GROUP
    highest = LOOKBACK + GROUP - 2
    offsets = list(range(lowest, highest + 1))
    raw_keys = jnp.dot(features, w_key, preferred_element_type=jnp.float32).reshape(
        row_count, kv_local, head_size
    )
    key_norm, key_inverse = rms_scale(raw_keys, k_gain)
    value_rows = (
        jnp.dot(features, w_value, preferred_element_type=jnp.float32)
        .astype(jnp.bfloat16)
        .reshape(row_count, kv_local, head_size)
    )
    encoded = jnp.stack([key_norm.astype(jnp.bfloat16), value_rows])
    pieces = {0: encoded}
    for offset in offsets:
        if offset != 0:
            pieces[offset] = from_behind(encoded, "seq", offset)
    gathered = jnp.stack([pieces[offset] for offset in offsets], axis=1)
    piece_count = len(offsets)
    encoders = seq_index - jnp.arange(lowest, highest + 1, dtype=jnp.int32)
    key_block = gathered[0].reshape(piece_count * row_count, kv_local, head_size)
    value_block = gathered[1].reshape(piece_count * row_count, kv_local, head_size)
    valid = (encoders >= 0) & (encoders < seq_count)
    all_slots = jnp.arange(slot_image.shape[0], dtype=jnp.int32)
    piece_ids = jnp.sum(
        jnp.where(encoders[:, None] == all_slots[None, :], slot_image[None, :], 0), axis=1
    )
    piece_tiles = jnp.sum(
        jnp.where(piece_ids[:, None] == all_slots[None, :], image_tiles[None, :], 0), axis=1
    )
    live_rows = valid[:, None] & (
        jnp.arange(row_count, dtype=jnp.int32)[None, :] < (piece_tiles * TILE_ROWS)[:, None]
    )
    key_ids = jnp.repeat(piece_ids, row_count)
    live_keys = live_rows.reshape(piece_count * row_count)
    block_tokens = tok_count // image_range.shape[0]
    range_first = jnp.repeat(image_range[:, 0], block_tokens)
    range_last = jnp.repeat(image_range[:, 1], block_tokens)
    key_mask = (
        (key_ids[None, :] >= range_first[:, None])
        & (key_ids[None, :] < range_last[:, None])
        & live_keys[None, :]
    )
    raw_query = queries.astype(jnp.float32).reshape(tok_count, kv_local, group_size, head_size)
    upstream = d_out.reshape(tok_count, kv_local, group_size, head_size)
    query_norm, query_inverse = rms_scale(raw_query, q_gain)
    query16 = query_norm.astype(jnp.bfloat16)
    scores = (
        jnp.einsum("tkgd,nkd->tkgn", query16, key_block, preferred_element_type=jnp.float32)
        * score_scale
    )
    exp_scores = jnp.where(key_mask[:, None, None, :], jnp.exp(scores), 0.0)
    denominator = jnp.sum(exp_scores, axis=-1, keepdims=True)
    has_image = jnp.any(key_mask, axis=-1)[:, None, None, None]
    attn_weights = exp_scores / jnp.where(has_image, denominator, 1.0)
    weights16 = attn_weights.astype(jnp.bfloat16)
    output_rows = jnp.einsum(
        "tkgn,nkd->tkgd", weights16, value_block, preferred_element_type=jnp.float32
    )
    grad_weights = jnp.einsum(
        "tkgd,nkd->tkgn", upstream, value_block, preferred_element_type=jnp.float32
    )
    row_delta = jnp.sum(attn_weights * grad_weights, axis=-1, keepdims=True)
    grad_scores = (attn_weights * (grad_weights - row_delta)).astype(jnp.bfloat16)
    grad_qnorm = (
        jnp.einsum("tkgn,nkd->tkgd", grad_scores, key_block, preferred_element_type=jnp.float32)
        * score_scale
    )
    grad_query = rms_back(raw_query, query_inverse, q_gain, grad_qnorm)
    key_grad = (
        jnp.einsum("tkgn,tkgd->nkd", grad_scores, query16, preferred_element_type=jnp.float32)
        * score_scale
    )
    value_grad = jnp.einsum(
        "tkgn,tkgd->nkd", weights16, upstream, preferred_element_type=jnp.float32
    )
    grads = jnp.stack([key_grad, value_grad]).reshape(
        2, piece_count, row_count, kv_local, head_size
    )
    returned = grads[:, -lowest]
    for offset in offsets:
        if offset != 0:
            returned = returned + from_behind(grads[:, offset - lowest], "seq", -offset)
    raw_grad = (
        rms_back(raw_keys, key_inverse, k_gain, returned[0])
        .reshape(row_count, kv_local * head_size)
        .astype(jnp.bfloat16)
    )
    value_grad16 = returned[1].reshape(row_count, kv_local * head_size).astype(jnp.bfloat16)
    contract = (((1,), (1,)), ((), ()))
    partial_sum = lax.dot_general(raw_grad, w_key, contract, preferred_element_type=jnp.float32)
    partial_sum = partial_sum + lax.dot_general(
        value_grad16, w_value, contract, preferred_element_type=jnp.float32
    )
    grad_features = lax.psum_scatter(
        partial_sum.astype(jnp.bfloat16), "tensor", scatter_dimension=1, tiled=True
    )
    attended = output_rows.astype(jnp.bfloat16).reshape(
        tok_count, kv_local * group_size * head_size
    )
    grad_queries = grad_query.astype(jnp.bfloat16).reshape(
        tok_count, kv_local * group_size * head_size
    )
    return (attended, grad_queries, grad_features)


def solution(mesh):
    in_specs = (
        P("seq", "tensor"),
        P("seq", None),
        P(None, "tensor"),
        P(None, "tensor"),
        P(),
        P(),
        P(),
        P(),
        P("seq", None),
        P("seq", "tensor"),
    )
    out_specs = (P("seq", "tensor"), P("seq", "tensor"), P("seq", "tensor"))
    return jax.shard_map(local, mesh=mesh, in_specs=in_specs, out_specs=out_specs, check_vma=False)
```

profile of v0, /device:TPU:2, one launch (start us, length us, event | category | flops | bytes accessed | tf_op | source)
XLA Modules:
  0.0 176.4 jit_solution(13870838331305238943)
XLA Ops:
  7.2 0.0 copy-start
  7.2 0.0 copy-start.4
  7.2 0.0 reduce-scatter.2.cloned.1.call-start
  7.2 1.9 %fusion.18 = bf16[1,96,1,128]{3,1,2,0:T(8,128)(2,1)S(1)} fusion(bf16[96,4096]{1,0:T(8,128)(2,1)} %param.11, bf16[4096,128]{1,0:T(8,128)(2,1)} %param.13), kind=kOutput, calls=%fused_computation.39 | convolution fusion | flops 100675584 | bytes 1859584 | tf_op jit(solution)/shard_map/dot_general | solution.py:48
  9.2 1.6 multiply_reduce_fusion.3
  10.8 0.7 fusion.60
  11.6 16.2 %collective-permute-start = (bf16[2,96,1,128]{3,1,0,2:T(8,128)(2,1)S(1)}, bf16[2,96,1,128]{3,1,0,2:T(8,128)(2,1)S(1)}, u32[]{:S(2)}, u32[]{:S(2)}) collective-permute-start(bf16[2,96,1,128]{3,1,0,2:T(8,128)(2,1)S(1)} %get-tuple-element.22), channel_id=1, source_target_pairs={{24,0},{32,8},{40,16},{48,24},{56,32},{64,40},{72,48},{80,56},{88,... | collective-permute-start | bytes 147464 | tf_op jit(solution)/shard_map/ppermute | solution.py:14
  27.7 1.9 %collective-permute-start.1 = (bf16[2,96,1,128]{3,1,0,2:T(8,128)(2,1)S(1)}, bf16[2,96,1,128]{3,1,0,2:T(8,128)(2,1)S(1)}, u32[]{:S(2)}, u32[]{:S(2)}) collective-permute-start(bf16[2,96,1,128]{3,1,0,2:T(8,128)(2,1)S(1)} %get-tuple-element.22), channel_id=1, source_target_pairs={{16,0},{24,8},{32,16},{40,24},{48,32},{56,40},{64,48},{72,56},{80,... | collective-permute-start | bytes 147464 | tf_op jit(solution)/shard_map/ppermute | solution.py:14
  29.7 2.5 %collective-permute-start.2 = (bf16[2,96,1,128]{3,1,0,2:T(8,128)(2,1)S(1)}, bf16[2,96,1,128]{3,1,0,2:T(8,128)(2,1)S(1)}, u32[]{:S(2)}, u32[]{:S(2)}) collective-permute-start(bf16[2,96,1,128]{3,1,0,2:T(8,128)(2,1)S(1)} %get-tuple-element.22), channel_id=1, source_target_pairs={{8,0},{16,8},{24,16},{32,24},{40,32},{48,40},{56,48},{64,56},{72,6... | collective-permute-start | bytes 147464 | tf_op jit(solution)/shard_map/ppermute | solution.py:14
  32.1 3.4 %collective-permute-start.3 = (bf16[2,96,1,128]{3,1,0,2:T(8,128)(2,1)S(1)}, bf16[2,96,1,128]{3,1,0,2:T(8,128)(2,1)S(1)}, u32[]{:S(2)}, u32[]{:S(2)}) collective-permute-start(bf16[2,96,1,128]{3,1,0,2:T(8,128)(2,1)S(1)} %get-tuple-element.22), channel_id=1, source_target_pairs={{0,8},{8,16},{16,24},{24,32},{32,40},{40,48},{48,56},{56,64},{64,7... | collective-permute-start | bytes 147464 | tf_op jit(solution)/shard_map/ppermute | solution.py:14
  35.5 4.8 %collective-permute-start.4 = (bf16[2,96,1,128]{3,1,0,2:T(8,128)(2,1)S(1)}, bf16[2,96,1,128]{3,1,0,2:T(8,128)(2,1)S(1)}, u32[]{:S(2)}, u32[]{:S(2)}) collective-permute-start(bf16[2,96,1,128]{3,1,0,2:T(8,128)(2,1)S(1)} %get-tuple-element.22), channel_id=1, source_target_pairs={{0,16},{8,24},{16,32},{24,40},{32,48},{40,56},{48,64},{56,72},{64,... | collective-permute-start | bytes 147464 | tf_op jit(solution)/shard_map/ppermute | solution.py:14
  40.4 0.8 select_reduce_fusion.1
  41.2 0.8 select_reduce_fusion
  42.1 0.1 fusion.68
  42.1 0.1 and.46
  42.2 0.8 slice_bitcast_fusion.2
  43.0 0.1 broadcast_in_dim.76
  43.1 0.1 lt.42
  43.2 0.1 broadcast_in_dim.75
  43.2 0.1 ge.30
  43.3 0.1 broadcast_in_dim.74
  43.4 0.1 ge.28
  43.5 1.2 copy.36
  44.7 0.1 multiply_reduce_fusion.1
  44.8 0.3 fusion.72
  45.1 0.7 broadcast_bitcast_fusion
  45.8 0.1 copy.47
  45.9 0.0 copy-start.7
  45.9 5.1 %collective-permute-start.5 = (bf16[2,96,1,128]{3,1,0,2:T(8,128)(2,1)S(1)}, bf16[2,96,1,128]{3,1,0,2:T(8,128)(2,1)S(1)}, u32[]{:S(2)}, u32[]{:S(2)}) collective-permute-start(bf16[2,96,1,128]{3,1,0,2:T(8,128)(2,1)S(1)} %get-tuple-element.22), channel_id=1, source_target_pairs={{0,24},{8,32},{16,40},{24,48},{32,56},{40,64},{48,72},{56,80},{64,... | collective-permute-start | bytes 147464 | tf_op jit(solution)/shard_map/ppermute | solution.py:14
  51.1 3.5 %collective-permute-start.6 = (bf16[2,96,1,128]{3,1,0,2:T(8,128)(2,1)S(1)}, bf16[2,96,1,128]{3,1,0,2:T(8,128)(2,1)S(1)}, u32[]{:S(2)}, u32[]{:S(2)}) collective-permute-start(bf16[2,96,1,128]{3,1,0,2:T(8,128)(2,1)S(1)} %get-tuple-element.22), channel_id=1, source_target_pairs={{0,32},{8,40},{16,48},{24,56},{32,64},{40,72},{48,80},{56,88},{64,... | collective-permute-start | bytes 147464 | tf_op jit(solution)/shard_map/ppermute | solution.py:14
  54.6 5.0 %collective-permute-start.7 = (bf16[2,96,1,128]{3,1,2,0:T(8,128)(2,1)S(1)}, bf16[2,96,1,128]{3,1,2,0:T(8,128)(2,1)S(1)}, u32[]{:S(2)}, u32[]{:S(2)}) collective-permute-start(bf16[2,96,1,128]{3,1,2,0:T(8,128)(2,1)S(1)} %get-tuple-element.21), channel_id=1, source_target_pairs={{0,40},{8,48},{16,56},{24,64},{32,72},{40,80},{48,88},{56,96},{64,... | collective-permute-start | bytes 147464 | tf_op jit(solution)/shard_map/ppermute | solution.py:14
  59.6 1.2 collective-permute-done.5
  60.9 6.0 %collective-permute-done.6 = bf16[2,96,1,128]{3,1,0,2:T(8,128)(2,1)S(1)} collective-permute-done((bf16[2,96,1,128]{3,1,0,2:T(8,128)(2,1)S(1)}, bf16[2,96,1,128]{3,1,0,2:T(8,128)(2,1)S(1)}, u32[]{:S(2)}, u32[]{:S(2)}) %collective-permute-start.6) | collective-permute-done | bytes 49184 | tf_op jit(solution)/shard_map/ppermute | solution.py:14
  66.9 2.8 %collective-permute-done.7 = bf16[2,96,1,128]{3,1,2,0:T(8,128)(2,1)S(1)} collective-permute-done((bf16[2,96,1,128]{3,1,2,0:T(8,128)(2,1)S(1)}, bf16[2,96,1,128]{3,1,2,0:T(8,128)(2,1)S(1)}, u32[]{:S(2)}, u32[]{:S(2)}) %collective-permute-start.7) | collective-permute-done | bytes 49184 | tf_op jit(solution)/shard_map/ppermute | solution.py:14
  69.7 0.3 mul.207.clone
  70.0 1.9 %fusion.4 = (f32[256,8]{0,1:T(8,128)S(1)}, f32[864,256,8]{1,0,2:T(8,128)S(1)}) fusion(pred[256,864]{0,1:T(8,128)(4,1)S(1)} %get-tuple-element.10, bf16[864,128,1]{1,0,2:T(8,128)(2,1)S(1)} %bitcast.231, f32[32,8,8,128]{3,2,1,0:T(8,128)S(1)} %bitcast.230, f32[1024]{0:T(1024)S(1)} %broadcast_bitcast_fusion, bf16[256,1024]{1,0:T(8,128)(2,1)S(1)} %copy-done.4), kind=kOutput, calls=%fused_computation.7 | convolution fusion | flops 459339776 | bytes 9105408 | tf_op jit(solution)/shard_map/tkgd,nkd->tkgn/dot_general | solution.py:88
  72.0 1.7 fusion.7
  73.7 2.1 %fusion = (f32[256,8]{0,1:T(8,128)S(1)}, f32[864,256,8]{1,0,2:T(8,128)S(1)}) fusion(f32[256,8]{0,1:T(8,128)S(1)} %broadcast_select_fusion, f32[864,256,8]{1,0,2:T(8,128)S(1)} %get-tuple-element.32, pred[256,864]{0,1:T(8,128)(4,1)S(1)} %get-tuple-element.10, bf16[864,128,1]{1,0,2:T(8,128)(2,1)S(1)} %bitcast.234, bf16[256,1024]{1,0:T(8,128)(2,1)S(1)} %copy-done.7), kind=kOutput, calls=%fused_computation.3 | convolution fusion | flops 461830144 | bytes 15138816 | tf_op jit(solution)/shard_map/tkgd,nkd->tkgn/dot_general | solution.py:99
  75.9 2.0 %fusion.6 = bf16[256,8,864]{0,2,1:T(8,128)(2,1)S(1)} fusion(f32[864,256,8]{1,0,2:T(8,128)S(1)} %get-tuple-element.34, f32[256,8]{0,1:T(8,128)S(1)} %get-tuple-element.33, f32[256,8]{0,1:T(8,128)S(1)} %broadcast_select_fusion, f32[864,256,8]{1,0,2:T(8,128)S(1)} %get-tuple-element.32, pred[256,864]{0,1:T(8,128)(4,1)S(1)} %get-tuple-element.10), kind=kLoop, calls=%fused_computation.10 | loop fusion | flops 10616832 | bytes 17932288 | tf_op jit(solution)/shard_map/reshape.30
  77.8 1.8 %copy-done.1 = bf16[256,8,864]{0,2,1:T(8,128)(2,1)} copy-done((bf16[256,8,864]{0,2,1:T(8,128)(2,1)}, bf16[256,8,864]{0,2,1:T(8,128)(2,1)S(1)}, u32[]{:S(2)}) %copy-start.1) | copy-done | bytes 3538968
  79.7 1.2 fusion.17
  80.8 0.1 fusion.47
  80.9 11.8 %collective-permute-start.15 = (f32[2,96,1,128]{3,1,2,0:T(8,128)S(1)}, f32[2,96,1,128]{3,1,2,0:T(8,128)S(1)}, u32[]{:S(2)}, u32[]{:S(2)}) collective-permute-start(f32[2,96,1,128]{3,1,2,0:T(8,128)S(1)} %get-tuple-element.17), channel_id=1, source_target_pairs={{40,0},{48,8},{56,16},{64,24},{72,32},{80,40},{88,48},{96,56},{104... | collective-permute-start | bytes 294920 | tf_op jit(solution)/shard_map/ppermute | solution.py:14
  92.7 1.9 %collective-permute-start.14 = (f32[2,96,1,128]{3,1,0,2:T(8,128)S(1)}, f32[2,96,1,128]{3,1,0,2:T(8,128)S(1)}, u32[]{:S(2)}, u32[]{:S(2)}) collective-permute-start(f32[2,96,1,128]{3,1,0,2:T(8,128)S(1)} %get-tuple-element.18), channel_id=1, source_target_pairs={{32,0},{40,8},{48,16},{56,24},{64,32},{72,40},{80,48},{88,56},{96,... | collective-permute-start | bytes 294920 | tf_op jit(solution)/shard_map/ppermute | solution.py:14
  94.6 3.6 %collective-permute-start.13 = (f32[2,96,1,128]{3,1,0,2:T(8,128)S(1)}, f32[2,96,1,128]{3,1,0,2:T(8,128)S(1)}, u32[]{:S(2)}, u32[]{:S(2)}) collective-permute-start(f32[2,96,1,128]{3,1,0,2:T(8,128)S(1)} %get-tuple-element.16), channel_id=1, source_target_pairs={{24,0},{32,8},{40,16},{48,24},{56,32},{64,40},{72,48},{80,56},{88,... | collective-permute-start | bytes 294920 | tf_op jit(solution)/shard_map/ppermute | solution.py:14
  98.2 3.1 %collective-permute-start.12 = (f32[2,96,1,128]{3,1,0,2:T(8,128)S(1)}, f32[2,96,1,128]{3,1,0,2:T(8,128)S(1)}, u32[]{:S(2)}, u32[]{:S(2)}) collective-permute-start(f32[2,96,1,128]{3,1,0,2:T(8,128)S(1)} %get-tuple-element.15), channel_id=1, source_target_pairs={{16,0},{24,8},{32,16},{40,24},{48,32},{56,40},{64,48},{72,56},{80,... | collective-permute-start | bytes 294920 | tf_op jit(solution)/shard_map/ppermute | solution.py:14
  101.3 2.8 %collective-permute-start.11 = (f32[2,96,1,128]{3,1,0,2:T(8,128)S(1)}, f32[2,96,1,128]{3,1,0,2:T(8,128)S(1)}, u32[]{:S(2)}, u32[]{:S(2)}) collective-permute-start(f32[2,96,1,128]{3,1,0,2:T(8,128)S(1)} %get-tuple-element.14), channel_id=1, source_target_pairs={{8,0},{16,8},{24,16},{32,24},{40,32},{48,40},{56,48},{64,56},{72,6... | collective-permute-start | bytes 294920 | tf_op jit(solution)/shard_map/ppermute | solution.py:14
  104.1 3.0 %collective-permute-start.10 = (f32[2,96,1,128]{3,1,0,2:T(8,128)S(1)}, f32[2,96,1,128]{3,1,0,2:T(8,128)S(1)}, u32[]{:S(2)}, u32[]{:S(2)}) collective-permute-start(f32[2,96,1,128]{3,1,0,2:T(8,128)S(1)} %get-tuple-element.13), channel_id=1, source_target_pairs={{0,8},{8,16},{16,24},{24,32},{32,40},{40,48},{48,56},{56,64},{64,7... | collective-permute-start | bytes 294920 | tf_op jit(solution)/shard_map/ppermute | solution.py:14
  107.1 4.3 %collective-permute-start.9 = (f32[2,96,1,128]{3,1,0,2:T(8,128)S(1)}, f32[2,96,1,128]{3,1,0,2:T(8,128)S(1)}, u32[]{:S(2)}, u32[]{:S(2)}) collective-permute-start(f32[2,96,1,128]{3,1,0,2:T(8,128)S(1)} %get-tuple-element.12), channel_id=1, source_target_pairs={{0,16},{8,24},{16,32},{24,40},{32,48},{40,56},{48,64},{56,72},{64,... | collective-permute-start | bytes 294920 | tf_op jit(solution)/shard_map/ppermute | solution.py:14
  111.4 6.2 %collective-permute-start.8 = (f32[2,96,1,128]{3,1,0,2:T(8,128)S(1)}, f32[2,96,1,128]{3,1,0,2:T(8,128)S(1)}, u32[]{:S(2)}, u32[]{:S(2)}) collective-permute-start(f32[2,96,1,128]{3,1,0,2:T(8,128)S(1)} %get-tuple-element.11), channel_id=1, source_target_pairs={{0,24},{8,32},{16,40},{24,48},{32,56},{40,64},{48,72},{56,80},{64,... | collective-permute-start | bytes 294920 | tf_op jit(solution)/shard_map/ppermute | solution.py:14
  117.7 2.2 %collective-permute-done.10 = f32[2,96,1,128]{3,1,0,2:T(8,128)S(1)} collective-permute-done((f32[2,96,1,128]{3,1,0,2:T(8,128)S(1)}, f32[2,96,1,128]{3,1,0,2:T(8,128)S(1)}, u32[]{:S(2)}, u32[]{:S(2)}) %collective-permute-start.10) | collective-permute-done | bytes 98336 | tf_op jit(solution)/shard_map/ppermute | solution.py:14
  119.9 4.0 %collective-permute-done.9 = f32[2,96,1,128]{3,1,0,2:T(8,128)S(1)} collective-permute-done((f32[2,96,1,128]{3,1,0,2:T(8,128)S(1)}, f32[2,96,1,128]{3,1,0,2:T(8,128)S(1)}, u32[]{:S(2)}, u32[]{:S(2)}) %collective-permute-start.9) | collective-permute-done | bytes 98336 | tf_op jit(solution)/shard_map/ppermute | solution.py:14
  124.0 2.7 %collective-permute-done.8 = f32[2,96,1,128]{3,1,0,2:T(8,128)S(1)} collective-permute-done((f32[2,96,1,128]{3,1,0,2:T(8,128)S(1)}, f32[2,96,1,128]{3,1,0,2:T(8,128)S(1)}, u32[]{:S(2)}, u32[]{:S(2)}) %collective-permute-start.8) | collective-permute-done | bytes 98336 | tf_op jit(solution)/shard_map/ppermute | solution.py:14
  126.7 0.1 bitcast_add_fusion
  126.7 0.1 multiply_reduce_fusion.2
  126.9 0.5 fusion.61
  127.4 1.4 fusion.5
  128.8 0.0 reduce-scatter.2.cloned.1.call-update
  128.8 4.8 %fusion.14 = bf16[128,256,8]{1,0,2:T(8,128)(2,1)S(1)} fusion(bf16[864,128,1]{1,0,2:T(8,128)(2,1)S(1)} %bitcast.235, f32[256,8]{0,1:T(8,128)S(1)} %broadcast_select_fusion, f32[864,256,8]{1,0,2:T(8,128)} %copy-done.2, pred[256,864]{0,1:T(8,128)(4,1)S(1)} %get-tuple-element.10), kind=kOutput, calls=%fused_computation.35 | convolution fusion | flops 460324864 | bytes 8052736 | tf_op jit(solution)/shard_map/tkgn,nkd->tkgd/dot_general | solution.py:96
  133.6 1.0 copy.43
  134.6 2.8 %multiply_reduce_fusion = (f32[256,8]{0,1:T(8,128)S(1)}, f32[256,1,8,128]{0,3,2,1:T(8,128)S(1)}) fusion(f32[256,1,8,128]{0,3,2,1:T(8,128)S(1)} %bitcast.224, f32[128]{0:T(128)S(1)} %broadcast_multiply_fusion.1, bf16[864,128,1]{1,0,2:T(8,128)(2,1)S(1)} %bitcast.232, bf16[256,8,864]{0,2,1:T(8,128)(2,1)} %copy-done.1), kind=kOutput, calls=%fused_computation.47 | convolution fusion | flops 453769216 | bytes 5865984 | tf_op jit(solution)/shard_map/tkgn,nkd->tkgd/dot_general | solution.py:105
  137.4 0.2 subtract_convert_fusion
  137.6 1.0 copy.44
  138.6 30.9 %reduce-scatter.2.cloned.1.call-done = bf16[96,512]{1,0:T(8,128)(2,1)} async-done(((bf16[96,4096]{1,0:T(8,128)(2,1)}), bf16[96,512]{1,0:T(8,128)(2,1)}) %reduce-scatter.2.cloned.1.call-update) | async-done | bytes 98320 | tf_op jit(solution)/shard_map/reduce_scatter | solution.py:134
  (42 shorter events, 0.2 us)
Async XLA Ops:
  7.2 2.0 %copy-start = (bf16[4096,128]{1,0:T(8,128)(2,1)S(1)}, bf16[4096,128]{1,0:T(8,128)(2,1)}, u32[]{:S(2)}) copy-start(bf16[4096,128]{1,0:T(8,128)(2,1)} %param.12) | copy-start | bytes 3145732
  7.2 62.9 %copy-start.4 = (bf16[256,1024]{1,0:T(8,128)(2,1)S(1)}, bf16[256,1024]{1,0:T(8,128)(2,1)}, u32[]{:S(2)}) copy-start(bf16[256,1024]{1,0:T(8,128)(2,1)} %param.10) | copy-start | bytes 1572868
  7.2 162.3 %reduce-scatter.2.cloned.1.call-start = ((), (), s32[]{:S(2)}) async-start(), calls=%async_computation.1 | async-start | bytes 884736 | tf_op jit(solution)/shard_map/reduce_scatter | solution.py:134
  11.6 34.4 %collective-permute-start = (bf16[2,96,1,128]{3,1,0,2:T(8,128)(2,1)S(1)}, bf16[2,96,1,128]{3,1,0,2:T(8,128)(2,1)S(1)}, u32[]{:S(2)}, u32[]{:S(2)}) collective-permute-start(bf16[2,96,1,128]{3,1,0,2:T(8,128)(2,1)S(1)} %get-tuple-element.22), channel_id=1, source_target_pairs={{24,0},{32,8},{40,16},{48,24},{56,32},{64,40},{72,48},{80,56},{88,... | collective-permute-start | bytes 147464 | tf_op jit(solution)/shard_map/ppermute | solution.py:14
  27.7 23.3 %collective-permute-start.1 = (bf16[2,96,1,128]{3,1,0,2:T(8,128)(2,1)S(1)}, bf16[2,96,1,128]{3,1,0,2:T(8,128)(2,1)S(1)}, u32[]{:S(2)}, u32[]{:S(2)}) collective-permute-start(bf16[2,96,1,128]{3,1,0,2:T(8,128)(2,1)S(1)} %get-tuple-element.22), channel_id=1, source_target_pairs={{16,0},{24,8},{32,16},{40,24},{48,32},{56,40},{64,48},{72,56},{80,... | collective-permute-start | bytes 147464 | tf_op jit(solution)/shard_map/ppermute | solution.py:14
  29.7 24.9 %collective-permute-start.2 = (bf16[2,96,1,128]{3,1,0,2:T(8,128)(2,1)S(1)}, bf16[2,96,1,128]{3,1,0,2:T(8,128)(2,1)S(1)}, u32[]{:S(2)}, u32[]{:S(2)}) collective-permute-start(bf16[2,96,1,128]{3,1,0,2:T(8,128)(2,1)S(1)} %get-tuple-element.22), channel_id=1, source_target_pairs={{8,0},{16,8},{24,16},{32,24},{40,32},{48,40},{56,48},{64,56},{72,6... | collective-permute-start | bytes 147464 | tf_op jit(solution)/shard_map/ppermute | solution.py:14
  32.1 27.4 %collective-permute-start.3 = (bf16[2,96,1,128]{3,1,0,2:T(8,128)(2,1)S(1)}, bf16[2,96,1,128]{3,1,0,2:T(8,128)(2,1)S(1)}, u32[]{:S(2)}, u32[]{:S(2)}) collective-permute-start(bf16[2,96,1,128]{3,1,0,2:T(8,128)(2,1)S(1)} %get-tuple-element.22), channel_id=1, source_target_pairs={{0,8},{8,16},{16,24},{24,32},{32,40},{40,48},{48,56},{56,64},{64,7... | collective-permute-start | bytes 147464 | tf_op jit(solution)/shard_map/ppermute | solution.py:14
  35.5 24.1 %collective-permute-start.4 = (bf16[2,96,1,128]{3,1,0,2:T(8,128)(2,1)S(1)}, bf16[2,96,1,128]{3,1,0,2:T(8,128)(2,1)S(1)}, u32[]{:S(2)}, u32[]{:S(2)}) collective-permute-start(bf16[2,96,1,128]{3,1,0,2:T(8,128)(2,1)S(1)} %get-tuple-element.22), channel_id=1, source_target_pairs={{0,16},{8,24},{16,32},{24,40},{32,48},{40,56},{48,64},{56,72},{64,... | collective-permute-start | bytes 147464 | tf_op jit(solution)/shard_map/ppermute | solution.py:14
  45.9 26.1 %copy-start.7 = (bf16[256,1024]{1,0:T(8,128)(2,1)S(1)}, bf16[256,1024]{1,0:T(8,128)(2,1)}, u32[]{:S(2)}) copy-start(bf16[256,1024]{1,0:T(8,128)(2,1)} %param.19) | copy-start | bytes 1572868
  45.9 14.9 %collective-permute-start.5 = (bf16[2,96,1,128]{3,1,0,2:T(8,128)(2,1)S(1)}, bf16[2,96,1,128]{3,1,0,2:T(8,128)(2,1)S(1)}, u32[]{:S(2)}, u32[]{:S(2)}) collective-permute-start(bf16[2,96,1,128]{3,1,0,2:T(8,128)(2,1)S(1)} %get-tuple-element.22), channel_id=1, source_target_pairs={{0,24},{8,32},{16,40},{24,48},{32,56},{40,64},{48,72},{56,80},{64,... | collective-permute-start | bytes 147464 | tf_op jit(solution)/shard_map/ppermute | solution.py:14
  51.1 15.8 %collective-permute-start.6 = (bf16[2,96,1,128]{3,1,0,2:T(8,128)(2,1)S(1)}, bf16[2,96,1,128]{3,1,0,2:T(8,128)(2,1)S(1)}, u32[]{:S(2)}, u32[]{:S(2)}) collective-permute-start(bf16[2,96,1,128]{3,1,0,2:T(8,128)(2,1)S(1)} %get-tuple-element.22), channel_id=1, source_target_pairs={{0,32},{8,40},{16,48},{24,56},{32,64},{40,72},{48,80},{56,88},{64,... | collective-permute-start | bytes 147464 | tf_op jit(solution)/shard_map/ppermute | solution.py:14
  54.6 15.1 %collective-permute-start.7 = (bf16[2,96,1,128]{3,1,2,0:T(8,128)(2,1)S(1)}, bf16[2,96,1,128]{3,1,2,0:T(8,128)(2,1)S(1)}, u32[]{:S(2)}, u32[]{:S(2)}) collective-permute-start(bf16[2,96,1,128]{3,1,2,0:T(8,128)(2,1)S(1)} %get-tuple-element.21), channel_id=1, source_target_pairs={{0,40},{8,48},{16,56},{24,64},{32,72},{40,80},{48,88},{56,96},{64,... | collective-permute-start | bytes 147464 | tf_op jit(solution)/shard_map/ppermute | solution.py:14
  72.0 3.9 %copy-start.2 = (f32[864,256,8]{1,0,2:T(8,128)}, f32[864,256,8]{1,0,2:T(8,128)S(1)}, u32[]{:S(2)}) copy-start(f32[864,256,8]{1,0,2:T(8,128)S(1)} %get-tuple-element.32) | copy-start | bytes 21233668
  75.8 3.8 %copy-start.6 = (f32[128]{0:T(128)S(1)}, f32[128]{0:T(128)}, u32[]{:S(2)}) copy-start(f32[128]{0:T(128)} %param.14) | copy-start | bytes 1540
  77.8 1.8 %copy-start.1 = (bf16[256,8,864]{0,2,1:T(8,128)(2,1)}, bf16[256,8,864]{0,2,1:T(8,128)(2,1)S(1)}, u32[]{:S(2)}) copy-start(bf16[256,8,864]{0,2,1:T(8,128)(2,1)S(1)} %fusion.6) | copy-start | bytes 10616836
  79.6 47.1 %copy-start.5 = (f32[128]{0:T(128)S(1)}, f32[128]{0:T(128)}, u32[]{:S(2)}) copy-start(f32[128]{0:T(128)} %param.15) | copy-start | bytes 1540
  79.7 47.7 %copy-start.3 = (bf16[4096,128]{1,0:T(8,128)(2,1)S(1)}, bf16[4096,128]{1,0:T(8,128)(2,1)}, u32[]{:S(2)}) copy-start(bf16[4096,128]{1,0:T(8,128)(2,1)} %param.13) | copy-start | bytes 3145732
  80.9 23.2 %collective-permute-start.15 = (f32[2,96,1,128]{3,1,2,0:T(8,128)S(1)}, f32[2,96,1,128]{3,1,2,0:T(8,128)S(1)}, u32[]{:S(2)}, u32[]{:S(2)}) collective-permute-start(f32[2,96,1,128]{3,1,2,0:T(8,128)S(1)} %get-tuple-element.17), channel_id=1, source_target_pairs={{40,0},{48,8},{56,16},{64,24},{72,32},{80,40},{88,48},{96,56},{104... | collective-permute-start | bytes 294920 | tf_op jit(solution)/shard_map/ppermute | solution.py:14
  92.7 14.5 %collective-permute-start.14 = (f32[2,96,1,128]{3,1,0,2:T(8,128)S(1)}, f32[2,96,1,128]{3,1,0,2:T(8,128)S(1)}, u32[]{:S(2)}, u32[]{:S(2)}) collective-permute-start(f32[2,96,1,128]{3,1,0,2:T(8,128)S(1)} %get-tuple-element.18), channel_id=1, source_target_pairs={{32,0},{40,8},{48,16},{56,24},{64,32},{72,40},{80,48},{88,56},{96,... | collective-permute-start | bytes 294920 | tf_op jit(solution)/shard_map/ppermute | solution.py:14
  94.6 16.8 %collective-permute-start.13 = (f32[2,96,1,128]{3,1,0,2:T(8,128)S(1)}, f32[2,96,1,128]{3,1,0,2:T(8,128)S(1)}, u32[]{:S(2)}, u32[]{:S(2)}) collective-permute-start(f32[2,96,1,128]{3,1,0,2:T(8,128)S(1)} %get-tuple-element.16), channel_id=1, source_target_pairs={{24,0},{32,8},{40,16},{48,24},{56,32},{64,40},{72,48},{80,56},{88,... | collective-permute-start | bytes 294920 | tf_op jit(solution)/shard_map/ppermute | solution.py:14
  98.2 19.5 %collective-permute-start.12 = (f32[2,96,1,128]{3,1,0,2:T(8,128)S(1)}, f32[2,96,1,128]{3,1,0,2:T(8,128)S(1)}, u32[]{:S(2)}, u32[]{:S(2)}) collective-permute-start(f32[2,96,1,128]{3,1,0,2:T(8,128)S(1)} %get-tuple-element.15), channel_id=1, source_target_pairs={{16,0},{24,8},{32,16},{40,24},{48,32},{56,40},{64,48},{72,56},{80,... | collective-permute-start | bytes 294920 | tf_op jit(solution)/shard_map/ppermute | solution.py:14
  101.3 16.4 %collective-permute-start.11 = (f32[2,96,1,128]{3,1,0,2:T(8,128)S(1)}, f32[2,96,1,128]{3,1,0,2:T(8,128)S(1)}, u32[]{:S(2)}, u32[]{:S(2)}) collective-permute-start(f32[2,96,1,128]{3,1,0,2:T(8,128)S(1)} %get-tuple-element.14), channel_id=1, source_target_pairs={{8,0},{16,8},{24,16},{32,24},{40,32},{48,40},{56,48},{64,56},{72,6... | collective-permute-start | bytes 294920 | tf_op jit(solution)/shard_map/ppermute | solution.py:14
  104.1 15.8 %collective-permute-start.10 = (f32[2,96,1,128]{3,1,0,2:T(8,128)S(1)}, f32[2,96,1,128]{3,1,0,2:T(8,128)S(1)}, u32[]{:S(2)}, u32[]{:S(2)}) collective-permute-start(f32[2,96,1,128]{3,1,0,2:T(8,128)S(1)} %get-tuple-element.13), channel_id=1, source_target_pairs={{0,8},{8,16},{16,24},{24,32},{32,40},{40,48},{48,56},{56,64},{64,7... | collective-permute-start | bytes 294920 | tf_op jit(solution)/shard_map/ppermute | solution.py:14
  107.1 16.8 %collective-permute-start.9 = (f32[2,96,1,128]{3,1,0,2:T(8,128)S(1)}, f32[2,96,1,128]{3,1,0,2:T(8,128)S(1)}, u32[]{:S(2)}, u32[]{:S(2)}) collective-permute-start(f32[2,96,1,128]{3,1,0,2:T(8,128)S(1)} %get-tuple-element.12), channel_id=1, source_target_pairs={{0,16},{8,24},{16,32},{24,40},{32,48},{40,56},{48,64},{56,72},{64,... | collective-permute-start | bytes 294920 | tf_op jit(solution)/shard_map/ppermute | solution.py:14
  111.4 15.2 %collective-permute-start.8 = (f32[2,96,1,128]{3,1,0,2:T(8,128)S(1)}, f32[2,96,1,128]{3,1,0,2:T(8,128)S(1)}, u32[]{:S(2)}, u32[]{:S(2)}) collective-permute-start(f32[2,96,1,128]{3,1,0,2:T(8,128)S(1)} %get-tuple-element.11), channel_id=1, source_target_pairs={{0,24},{8,32},{16,40},{24,48},{32,56},{40,64},{48,72},{56,80},{64,... | collective-permute-start | bytes 294920 | tf_op jit(solution)/shard_map/ppermute | solution.py:14
Sparse Core Ops, SparseCore 0:
  128.9 40.5 reduce-scatter.1
where the time goes:
time: 177 us; the launch traced here: 176 us
  starting transfers between devices  78.9 us (45%)
  waiting for transfers between devices  49.9 us (28%)
  matrix products  19.9 us (11%)
  between operations  14.6 us (8%)
  local copies, waits for them, and re-layouts  7.64 us (4%)
  other arithmetic  5.38 us (3%)
    ppermute x16, starting transfers between devices, from_behind(): return lax.ppermute(array, axis, pairs)  78.9 us
    reduce_scatter x1, waiting for transfers between devices, local(): lax.psum_scatter(partial_sum.astype(jnp.bfloat16), 'tensor', scatter_dime...  30.9 us
    ppermute x16, waiting for transfers between devices, from_behind(): return lax.ppermute(array, axis, pairs)  19 us
    dot_general x1, matrix products, local(): jnp.einsum('tkgn,nkd->tkgd', weights16, value_block, preferred_element_ty...  4.83 us
    unnamed x26, local copies, waits for them, and re-layouts  4.06 us
  transfers between devices with their start and end apart: 17, of which 7 were waited for; matrix products, arithmetic and copies ran while one was open for 9% of the time, Pallas kernels for 0%

commit v1 on v0

v1 whole, which is shorter than its diff:
```python
import functools

import jax
import jax.numpy as jnp
from jax import lax
from jax.experimental import pallas as pl
from jax.experimental.pallas import tpu as pltpu
from jax.sharding import PartitionSpec as P

TILE_ROWS = 24
GROUP = 4
LOOKBACK = 3
BF16 = jnp.bfloat16
F32 = jnp.float32
MESH = pl.DeviceIdType.MESH
LOG2E = 1.4426950408889634
HIDDEN = -1e30
W_CHUNKS = 4


def dot(a, b, contract):
    return lax.dot_general(a, b, (contract, ((), ())), preferred_element_type=F32)


def kernel(
    seq_count, tensor_count,
    q_hbm, f_hbm, wk_hbm, wv_hbm, qg_ref, kg_ref, slot_ref, tiles_ref, range_ref, do_hbm,
    att_hbm, gq_hbm, gf_hbm,
    f_v, w_v, q_v, do_v, att_v, gq_v, gf_v,
    raw_v, kv_in, kcat, q16_v, qt_v, inv_v, bias_v, p_v, ds_v,
    g_v, gsend, grecv, csend, crecv, rrecv, a_v,
    psend, precv, bsend, brecv,
    load_sem, store_sem, kv_send, kv_recv, relay_sem, g_send, g_recv, c_send, c_recv,
    rg_send, rg_recv, p_send, p_recv, b_send, b_recv,
):
    s = lax.axis_index("seq")
    t = lax.axis_index("tensor")
    g = s // GROUP
    m = s % GROUP
    base = g * GROUP
    chip = t // 2
    core = t % 2
    chips = tensor_count // 2
    groups = seq_count // GROUP
    rows, width = f_v.shape
    head = qg_ref.shape[1]
    toks = q_v.shape[0]
    heads = q_v.shape[1] // head
    scale = head ** (-0.5)
    has_next = g < groups - 1
    has_prev = g > 0
    partner = (s, t + 1 - 2 * core)

    step = width // W_CHUNKS
    loads = []
    for i in range(W_CHUNKS):
        part = pl.ds(i * step, step)
        loads.append([
            pltpu.make_async_copy(f_hbm.at[:, part], f_v.at[:, part], load_sem.at[3 * i]),
            pltpu.make_async_copy(wk_hbm.at[part, :], w_v.at[part, pl.ds(0, head)], load_sem.at[3 * i + 1]),
            pltpu.make_async_copy(wv_hbm.at[part, :], w_v.at[part, pl.ds(head, head)], load_sem.at[3 * i + 2]),
        ])
    q_load = pltpu.make_async_copy(q_hbm, q_v, load_sem.at[3 * W_CHUNKS])
    do_load = pltpu.make_async_copy(do_hbm, do_v, load_sem.at[3 * W_CHUNKS + 1])
    for group_loads in loads:
        for copy in group_loads:
            copy.start()
    q_load.start()
    do_load.start()

    barrier = pltpu.get_barrier_semaphore()

    def greet(device):
        pl.semaphore_signal(barrier, inc=1, device_id=device, device_id_type=MESH)

    for off in range(1, GROUP):
        greet((base + (m + off) % GROUP, t))
    greet(partner)
    for off in range(1, chips):
        greet((s, ((chip + off) % chips) * 2 + core))

    @pl.when(has_next)
    def _():
        greet((base + GROUP, t))

    @pl.when(has_next & (m == GROUP - 1))
    def _():
        greet((base + GROUP + 1, t))

    @pl.when(has_prev & (m == 0))
    def _():
        for e in range(GROUP):
            greet((base - GROUP + e, t))

    @pl.when(has_prev & (m == 1))
    def _():
        greet((base - 1, t))

    acc = jnp.zeros((rows, 2 * head), F32)
    for i in range(W_CHUNKS):
        for copy in loads[i]:
            copy.wait()
        part = slice(i * step, (i + 1) * step)
        acc = acc + dot(f_v[:, part], w_v[part, :], ((1,), (0,)))
    raw = acc[:, :head]
    raw_v[...] = raw
    kinv = lax.rsqrt(jnp.mean(raw * raw, axis=-1, keepdims=True) + 1e-05)
    kv_in[m, :, :head] = (raw * kinv * kg_ref[...]).astype(BF16)
    kv_in[m, :, head:] = acc[:, head:].astype(BF16)

    peers = (
        GROUP - 1 + chips
        + jnp.where(has_next, 1, 0)
        + jnp.where(has_next & (m == GROUP - 1), 1, 0)
        + jnp.where(has_prev & (m == 0), GROUP, 0)
        + jnp.where(has_prev & (m == 1), 1, 0)
    )
    pl.semaphore_wait(barrier, peers)

    def remote(src, dst, send, recv, device):
        return pltpu.make_async_remote_copy(
            src_ref=src, dst_ref=dst, send_sem=send, recv_sem=recv,
            device_id=device, device_id_type=MESH,
        )

    def kv_cross():
        return remote(
            kv_in.at[m], kv_in.at[GROUP + m], kv_send.at[GROUP - 1], kv_recv.at[GROUP + m],
            (base + GROUP, t),
        )

    def kv_group(off):
        return remote(
            kv_in.at[m], kv_in.at[m], kv_send.at[off - 1], kv_recv.at[m],
            (base + (m + off) % GROUP, t),
        )

    def kv_arrived(slot):
        pltpu.make_async_copy(kv_in.at[slot], kv_in.at[slot], kv_recv.at[slot]).wait()

    @pl.when(has_next)
    def _():
        kv_cross().start()

    for off in range(1, GROUP):
        kv_group(off).start()

    q_load.wait()
    for h in range(heads):
        cols = slice(h * head, (h + 1) * head)
        x = q_v[:, cols].astype(F32)
        inv = lax.rsqrt(jnp.mean(x * x, axis=-1, keepdims=True) + 1e-05)
        inv_v[h] = jnp.broadcast_to(inv, (toks, head))
        normed = (x * inv * qg_ref[...]).astype(BF16)
        q16_v[:, cols] = normed
        qt_v[h] = normed.astype(F32).T.astype(BF16)

    blocks = range_ref.shape[0]
    per_block = toks // blocks
    block_of = lax.broadcasted_iota(jnp.int32, (1, toks), 1) // per_block
    row_of = lax.broadcasted_iota(jnp.int32, (rows, toks), 0)
    for j in range(LOOKBACK):
        image = s - (LOOKBACK - 1) + j
        live = tiles_ref[jnp.maximum(image, 0)] * TILE_ROWS
        limit = jnp.zeros((1, toks), jnp.int32)
        for b in range(blocks):
            seen = (range_ref[b, 0] <= image) & (image < range_ref[b, 1])
            limit = jnp.where(block_of == b, jnp.where(seen, live, 0), limit)
        bias_v[j * rows:(j + 1) * rows, :] = jnp.where(row_of < limit, 0.0, HIDDEN)
    do_load.wait()

    for off in range(1, GROUP):
        kv_arrived((m + off) % GROUP)
    ids = [slot_ref[base + e] for e in range(GROUP)]
    for j in range(LOOKBACK):
        image = s - (LOOKBACK - 1) + j
        chosen = jnp.zeros((rows, 2 * head), BF16)
        for e in range(GROUP):
            chosen = jnp.where(ids[e] == image, kv_in[e], chosen)
        kcat[j * rows:(j + 1) * rows, :] = chosen

    last = pl.ds((LOOKBACK - 1) * rows, rows)

    def kv_relay():
        return remote(
            kcat.at[last], kv_in.at[GROUP], relay_sem, kv_recv.at[GROUP], (base + GROUP + 1, t)
        )

    @pl.when(has_next & (m == GROUP - 1))
    def _():
        kv_relay().start()

    @pl.when(has_prev & (m == 0))
    def _():
        for e in range(GROUP):
            kv_arrived(GROUP + e)
        for j in range(LOOKBACK - 1):
            image = s - (LOOKBACK - 1) + j
            chosen = jnp.zeros((rows, 2 * head), BF16)
            for e in range(GROUP):
                chosen = jnp.where(slot_ref[base - GROUP + e] == image, kv_in[GROUP + e], chosen)
            kcat[j * rows:(j + 1) * rows, :] = chosen

    @pl.when(has_prev & (m == 1))
    def _():
        kv_arrived(GROUP)
        kcat[:rows, :] = kv_in[GROUP]

    keys = kcat[:, :head]
    values = kcat[:, head:]
    for h in range(heads):
        cols = slice(h * head, (h + 1) * head)
        scores = dot(keys, qt_v[h], ((1,), (0,)))
        e = jnp.exp2(scores * (scale * LOG2E) + bias_v[...])
        total = jnp.sum(e, axis=0, keepdims=True)
        p = e * jnp.where(total > 0.0, 1.0 / total, 0.0)
        p_v[h] = p.astype(BF16)
        dp = dot(values, do_v[:, cols], ((1,), (1,)))
        delta = jnp.sum(p * dp, axis=0, keepdims=True)
        ds_v[h] = (p * (dp - delta)).astype(BF16)

    for j in range(LOOKBACK):
        part = slice(j * rows, (j + 1) * rows)
        dk = jnp.zeros((rows, head), F32)
        dv = jnp.zeros((rows, head), F32)
        for h in range(heads):
            cols = slice(h * head, (h + 1) * head)
            dk = dk + dot(ds_v[h, part, :], q16_v[:, cols], ((1,), (0,)))
            dv = dv + dot(p_v[h, part, :], do_v[:, cols], ((1,), (0,)))
        g_v[j, :, :head] = dk * scale
        g_v[j, :, head:] = dv

    def for_slot(image_id, count):
        total = jnp.zeros((rows, 2 * head), F32)
        for j in range(count):
            total = jnp.where(image_id == s - (LOOKBACK - 1) + j, g_v[j], total)
        return total

    def cross_back(e):
        return remote(csend.at[e], crecv, c_send.at[e], c_recv, (base - GROUP + e, t))

    def relay_back():
        return remote(csend.at[0], rrecv, rg_send, rg_recv, (base - 1, t))

    @pl.when(has_prev & (m == 0))
    def _():
        for e in range(GROUP):
            csend[e] = for_slot(slot_ref[base - GROUP + e], LOOKBACK - 1).astype(BF16)
            cross_back(e).start()

    @pl.when(has_prev & (m == 1))
    def _():
        csend[0] = g_v[0].astype(BF16)
        relay_back().start()

    @pl.when(has_next & (m == GROUP - 1))
    def _():
        pltpu.make_async_copy(rrecv, rrecv, rg_recv).wait()
        g_v[LOOKBACK - 1] = g_v[LOOKBACK - 1] + rrecv[...].astype(F32)

    def group_back(off):
        return remote(
            gsend.at[off - 1], grecv.at[off - 1], g_send.at[off - 1], g_recv.at[off - 1],
            (base + (m + off) % GROUP, t),
        )

    for off in range(1, GROUP):
        gsend[off - 1] = for_slot(slot_ref[base + (m + off) % GROUP], LOOKBACK).astype(BF16)
        group_back(off).start()

    for h in range(heads):
        cols = slice(h * head, (h + 1) * head)
        att_v[:, cols] = dot(p_v[h], values, ((0,), (0,))).astype(BF16)
        x = q_v[:, cols].astype(F32)
        inv = inv_v[h]
        up = dot(ds_v[h], keys, ((0,), (0,))) * (qg_ref[...] * scale)
        mean = jnp.mean(up * x, axis=-1, keepdims=True)
        gq_v[:, cols] = (inv * up - x * (inv * inv * inv) * mean).astype(BF16)
    att_store = pltpu.make_async_copy(att_v, att_hbm, store_sem.at[0])
    gq_store = pltpu.make_async_copy(gq_v, gq_hbm, store_sem.at[1])
    att_store.start()
    gq_store.start()

    mine = for_slot(slot_ref[s], LOOKBACK)
    g_v[0] = mine
    for off in range(1, GROUP):
        group_back(off).wait_recv()
        g_v[0] = g_v[0] + grecv[off - 1].astype(F32)

    @pl.when(has_next)
    def _():
        pltpu.make_async_copy(crecv, crecv, c_recv).wait()
        g_v[0] = g_v[0] + crecv[...].astype(F32)

    raw = raw_v[...]
    kinv = lax.rsqrt(jnp.mean(raw * raw, axis=-1, keepdims=True) + 1e-05)
    up = g_v[0, :, :head] * kg_ref[...]
    mean = jnp.mean(up * raw, axis=-1, keepdims=True)
    a_v[:, :head] = (kinv * up - raw * (kinv * kinv * kinv) * mean).astype(BF16)
    a_v[:, head:] = g_v[0, :, head:].astype(BF16)

    out_cols = gf_v.shape[1]

    def term(owner):
        part = pl.ds(pl.multiple_of(owner * out_cols, out_cols), out_cols)
        return dot(a_v[...], w_v[part, :], ((1,), (1,)))

    def to_partner(i):
        return remote(psend.at[i], precv.at[i], p_send.at[i], p_recv.at[i], partner)

    def to_chip(i):
        return remote(
            bsend.at[i - 1], brecv.at[i - 1], b_send.at[i - 1], b_recv.at[i - 1],
            (s, ((chip + i) % chips) * 2 + core),
        )

    order = list(range(1, chips)) + [0]
    for i in order:
        psend[i] = term(((chip + i) % chips) * 2 + 1 - core).astype(BF16)
        to_partner(i).start()
    for i in order:
        own = term(((chip + i) % chips) * 2 + core).astype(BF16).astype(F32)
        to_partner(i).wait_recv()
        both = own + precv[i].astype(F32)
        if i:
            bsend[i - 1] = both.astype(BF16)
            to_chip(i).start()
    for i in range(1, chips):
        to_chip(i).wait_recv()
        both = both + brecv[i - 1].astype(F32)
    gf_v[...] = both.astype(BF16)
    gf_store = pltpu.make_async_copy(gf_v, gf_hbm, store_sem.at[2])
    gf_store.start()

    for off in range(1, GROUP):
        kv_group(off).wait_send()
        group_back(off).wait_send()

    @pl.when(has_next)
    def _():
        kv_cross().wait_send()

    @pl.when(has_next & (m == GROUP - 1))
    def _():
        kv_relay().wait_send()

    @pl.when(has_prev & (m == 0))
    def _():
        for e in range(GROUP):
            cross_back(e).wait_send()

    @pl.when(has_prev & (m == 1))
    def _():
        relay_back().wait_send()

    for i in range(chips):
        to_partner(i).wait_send()
    for i in range(1, chips):
        to_chip(i).wait_send()
    att_store.wait()
    gq_store.wait()
    gf_store.wait()


def local(
    queries, features, w_key, w_value, q_gain, k_gain, slot_image, image_tiles, image_range, d_out
):
    seq_count = lax.axis_size("seq")
    tensor_count = lax.axis_size("tensor")
    chips = tensor_count // 2
    toks, q_cols = queries.shape
    rows, width = features.shape
    head = q_gain.shape[0]
    heads = q_cols // head
    keys = LOOKBACK * rows
    out_cols = width // tensor_count
    dma = pltpu.SemaphoreType.DMA
    any_space = pl.BlockSpec(memory_space=pl.ANY)
    vmem = pl.BlockSpec(memory_space=pltpu.VMEM)
    smem = pl.BlockSpec(memory_space=pltpu.SMEM)
    scratch = [
        pltpu.VMEM((rows, width), BF16),
        pltpu.VMEM((width, 2 * head), BF16),
        pltpu.VMEM((toks, q_cols), BF16),
        pltpu.VMEM((toks, q_cols), BF16),
        pltpu.VMEM((toks, q_cols), BF16),
        pltpu.VMEM((toks, q_cols), BF16),
        pltpu.VMEM((rows, out_cols), BF16),
        pltpu.VMEM((rows, head), F32),
        pltpu.VMEM((2 * GROUP, rows, 2 * head), BF16),
        pltpu.VMEM((keys, 2 * head), BF16),
        pltpu.VMEM((toks, q_cols), BF16),
        pltpu.VMEM((heads, head, toks), BF16),
        pltpu.VMEM((heads, toks, head), F32),
        pltpu.VMEM((keys, toks), F32),
        pltpu.VMEM((heads, keys, toks), BF16),
        pltpu.VMEM((heads, keys, toks), BF16),
        pltpu.VMEM((LOOKBACK, rows, 2 * head), F32),
        pltpu.VMEM((GROUP - 1, rows, 2 * head), BF16),
        pltpu.VMEM((GROUP - 1, rows, 2 * head), BF16),
        pltpu.VMEM((GROUP, rows, 2 * head), BF16),
        pltpu.VMEM((rows, 2 * head), BF16),
        pltpu.VMEM((rows, 2 * head), BF16),
        pltpu.VMEM((rows, 2 * head), BF16),
        pltpu.VMEM((chips, rows, out_cols), BF16),
        pltpu.VMEM((chips, rows, out_cols), BF16),
        pltpu.VMEM((chips - 1, rows, out_cols), BF16),
        pltpu.VMEM((chips - 1, rows, out_cols), BF16),
        dma((3 * W_CHUNKS + 2,)),
        dma((3,)),
        dma((GROUP,)),
        dma((2 * GROUP,)),
        dma,
        dma((GROUP - 1,)),
        dma((GROUP - 1,)),
        dma((GROUP,)),
        dma,
        dma,
        dma,
        dma((chips,)),
        dma((chips,)),
        dma((chips - 1,)),
        dma((chips - 1,)),
    ]
    return pl.pallas_call(
        functools.partial(kernel, seq_count, tensor_count),
        out_shape=(
            jax.ShapeDtypeStruct((toks, q_cols), BF16),
            jax.ShapeDtypeStruct((toks, q_cols), BF16),
            jax.ShapeDtypeStruct((rows, out_cols), BF16),
        ),
        in_specs=[any_space] * 4 + [vmem] * 2 + [smem] * 3 + [any_space],
        out_specs=(any_space,) * 3,
        scratch_shapes=scratch,
        compiler_params=pltpu.CompilerParams(
            collective_id=0, has_side_effects=True, vmem_limit_bytes=48 * 1024 * 1024
        ),
        cost_estimate=pl.CostEstimate(
            flops=1_300_000_000, bytes_accessed=5_500_000, transcendentals=600_000
        ),
    )(
        queries, features, w_key, w_value, q_gain.reshape(1, head), k_gain.reshape(1, head),
        slot_image, image_tiles, image_range, d_out,
    )


def solution(mesh):
    in_specs = (
        P("seq", "tensor"),
        P("seq", None),
        P(None, "tensor"),
        P(None, "tensor"),
        P(),
        P(),
        P(),
        P(),
        P("seq", None),
        P("seq", "tensor"),
    )
    out_specs = (P("seq", "tensor"), P("seq", "tensor"), P("seq", "tensor"))
    return jax.shard_map(local, mesh=mesh, in_specs=in_specs, out_specs=out_specs, check_vma=False)
```

time: 177 us -> 61.6 us (0.35)
  the two profiles are of different devices: /device:TPU:2 before, /device:TPU:15 now
where the time goes in v1:
time: 61.6 us; the launch traced here: 61.2 us
  Pallas kernels  51.3 us (83%)
  local copies, waits for them, and re-layouts  9.26 us (15%)
  between operations  0.66 us (1%)
    pallas_call x1, Pallas kernels, local(): pl.pallas_call(functools.partial(kernel, seq_count, tensor_count), out_sh...  51.3 us
    unnamed x24, local copies, waits for them, and re-layouts  9.26 us

profile of v1, /device:TPU:15, one launch (start us, length us, event | category | flops | bytes accessed | tf_op | source)
XLA Modules:
  0.0 61.2 jit_solution(17357171718557666372)
XLA Ops:
  0.6 0.0 copy-start.9
  0.6 0.7 %copy-done.9 = s32[4,2]{0,1:T(2,128)S(1)} copy-done((s32[4,2]{0,1:T(2,128)S(1)}, s32[4,2]{0,1:T(2,128)}, u32[]{:S(2)}) %copy-start.9) | copy-done | bytes 56
  1.3 0.0 copy-start.5
  1.3 0.0 copy-start.6
  1.3 0.0 copy-start.7
  1.3 0.0 copy-start.8
  1.3 0.1 copy.13.range_ref
  1.4 0.6 copy-done.5
  2.0 0.0 copy-done.6
  2.0 0.0 copy-done.7
  2.0 0.0 copy-done.8
  2.0 0.0 copy-start
  2.0 1.2 %copy-done = bf16[4096,128]{1,0:T(8,128)(2,1)S(1)} copy-done((bf16[4096,128]{1,0:T(8,128)(2,1)S(1)}, bf16[4096,128]{1,0:T(8,128)(2,1)}, u32[]{:S(2)}) %copy-start) | copy-done | bytes 1048600
  3.2 0.0 copy-start.1
  3.2 1.2 %copy-done.1 = bf16[4096,128]{1,0:T(8,128)(2,1)S(1)} copy-done((bf16[4096,128]{1,0:T(8,128)(2,1)S(1)}, bf16[4096,128]{1,0:T(8,128)(2,1)}, u32[]{:S(2)}) %copy-start.1) | copy-done | bytes 1048600
  4.5 0.0 copy-start.2
  4.5 1.1 %copy-done.2 = bf16[96,4096]{1,0:T(8,128)(2,1)S(1)} copy-done((bf16[96,4096]{1,0:T(8,128)(2,1)S(1)}, bf16[96,4096]{1,0:T(8,128)(2,1)}, u32[]{:S(2)}) %copy-start.2) | copy-done | bytes 786456
  5.6 0.0 copy-start.3
  5.6 1.0 %copy-done.3 = bf16[256,1024]{1,0:T(8,128)(2,1)S(1)} copy-done((bf16[256,1024]{1,0:T(8,128)(2,1)S(1)}, bf16[256,1024]{1,0:T(8,128)(2,1)}, u32[]{:S(2)}) %copy-start.3) | copy-done | bytes 524312
  6.6 0.0 copy-start.4
  6.6 1.0 %copy-done.4 = bf16[256,1024]{1,0:T(8,128)(2,1)S(1)} copy-done((bf16[256,1024]{1,0:T(8,128)(2,1)S(1)}, bf16[256,1024]{1,0:T(8,128)(2,1)}, u32[]{:S(2)}) %copy-start.4) | copy-done | bytes 524312
  7.7 51.3 %shard_map.121 = (bf16[256,1024]{1,0:T(8,128)(2,1)S(1)}, bf16[256,1024]{1,0:T(8,128)(2,1)S(1)}, bf16[96,512]{1,0:T(8,128)(2,1)S(1)}) custom-call(bf16[256,1024]{1,0:T(8,128)(2,1)S(1)} %copy-done.3, bf16[96,4096]{1,0:T(8,128)(2,1)S(1)} %copy-done.2, bf16[4096,128]{1,0:T(8,128)(2,1)S(1)} %copy-done, bf16[4096,128]{1,0:T(8,128)(2,1)S(1)} %copy-done.1, ...), custom_call_target="tpu_custom_call" | custom-call | flops 1300000000 | bytes 5500000 | tf_op jit(solution)/shard_map/pallas_call | solution.py:425
  59.0 0.8 %copy.17 = bf16[256,1024]{1,0:T(8,128)(2,1)} copy(bf16[256,1024]{1,0:T(8,128)(2,1)S(1)} %get-tuple-element.6) | data formatting | bytes 1048576
  59.8 0.8 %copy.18 = bf16[256,1024]{1,0:T(8,128)(2,1)} copy(bf16[256,1024]{1,0:T(8,128)(2,1)S(1)} %get-tuple-element.7) | data formatting | bytes 1048576
  60.6 0.6 %copy.19 = bf16[96,512]{1,0:T(8,128)(2,1)} copy(bf16[96,512]{1,0:T(8,128)(2,1)S(1)} %get-tuple-element.8) | data formatting | bytes 196608
Async XLA Ops:
  0.6 0.7 %copy-start.9 = (s32[4,2]{0,1:T(2,128)S(1)}, s32[4,2]{0,1:T(2,128)}, u32[]{:S(2)}) copy-start(s32[4,2]{0,1:T(2,128)} %param.18) | copy-start | bytes 100
  1.3 0.7 %copy-start.5 = (f32[128]{0:T(128)S(1)}, f32[128]{0:T(128)}, u32[]{:S(2)}) copy-start(f32[128]{0:T(128)} %param.14) | copy-start | bytes 1540
  1.3 0.7 %copy-start.6 = (f32[128]{0:T(128)S(1)}, f32[128]{0:T(128)}, u32[]{:S(2)}) copy-start(f32[128]{0:T(128)} %param.15) | copy-start | bytes 1540
  1.3 0.7 %copy-start.7 = (s32[64]{0:T(128)S(1)}, s32[64]{0:T(128)}, u32[]{:S(2)}) copy-start(s32[64]{0:T(128)} %slot_ref.1) | copy-start | bytes 772
  1.3 0.7 %copy-start.8 = (s32[64]{0:T(128)S(1)}, s32[64]{0:T(128)}, u32[]{:S(2)}) copy-start(s32[64]{0:T(128)} %tiles_ref.1) | copy-start | bytes 772
  2.0 1.2 %copy-start = (bf16[4096,128]{1,0:T(8,128)(2,1)S(1)}, bf16[4096,128]{1,0:T(8,128)(2,1)}, u32[]{:S(2)}) copy-start(bf16[4096,128]{1,0:T(8,128)(2,1)} %wk_hbm.1) | copy-start | bytes 3145732
  3.2 1.2 %copy-start.1 = (bf16[4096,128]{1,0:T(8,128)(2,1)S(1)}, bf16[4096,128]{1,0:T(8,128)(2,1)}, u32[]{:S(2)}) copy-start(bf16[4096,128]{1,0:T(8,128)(2,1)} %wv_hbm.1) | copy-start | bytes 3145732
  4.5 1.1 %copy-start.2 = (bf16[96,4096]{1,0:T(8,128)(2,1)S(1)}, bf16[96,4096]{1,0:T(8,128)(2,1)}, u32[]{:S(2)}) copy-start(bf16[96,4096]{1,0:T(8,128)(2,1)} %f_hbm.1) | copy-start | bytes 2359300
  5.6 1.0 %copy-start.3 = (bf16[256,1024]{1,0:T(8,128)(2,1)S(1)}, bf16[256,1024]{1,0:T(8,128)(2,1)}, u32[]{:S(2)}) copy-start(bf16[256,1024]{1,0:T(8,128)(2,1)} %q_hbm.1) | copy-start | bytes 1572868
  6.6 1.0 %copy-start.4 = (bf16[256,1024]{1,0:T(8,128)(2,1)S(1)}, bf16[256,1024]{1,0:T(8,128)(2,1)}, u32[]{:S(2)}) copy-start(bf16[256,1024]{1,0:T(8,128)(2,1)} %do_hbm.1) | copy-start | bytes 1572868

commit v2 on v1

--- a/solution.py
+++ b/solution.py
@@ -24,14 +24,15 @@
 
 def kernel(
     seq_count, tensor_count,
-    q_hbm, f_hbm, wk_hbm, wv_hbm, qg_ref, kg_ref, slot_ref, tiles_ref, range_ref, do_hbm,
+    q_hbm, f_hbm, wk_hbm, wv_hbm, qg_hbm, kg_hbm, slot_hbm, tiles_hbm, range_hbm, do_hbm,
     att_hbm, gq_hbm, gf_hbm,
+    qg_ref, kg_ref, slot_ref, tiles_ref, range_ref,
     f_v, w_v, q_v, do_v, att_v, gq_v, gf_v,
     raw_v, kv_in, kcat, q16_v, qt_v, inv_v, bias_v, p_v, ds_v,
-    g_v, gsend, grecv, csend, crecv, rrecv, a_v,
-    psend, precv, bsend, brecv,
-    load_sem, store_sem, kv_send, kv_recv, relay_sem, g_send, g_recv, c_send, c_recv,
-    rg_send, rg_recv, p_send, p_recv, b_send, b_recv,
+    g_v, gsend, grecv, csend, crecv, a_v,
+    psend, precv, bsend, brecv, sum_v,
+    small_sem, load_sem, store_sem, kv_send, kv_recv, g_send, g_recv, c_send, c_recv,
+    p_send, p_recv, b_send, b_recv,
 ):
     s = lax.axis_index("seq")
     t = lax.axis_index("tensor")
@@ -49,7 +50,45 @@
     scale = head ** (-0.5)
     has_next = g < groups - 1
     has_prev = g > 0
+    follows = has_prev & (m < 2)
+    inner = (chip % 3 + 1) // 2
     partner = (s, t + 1 - 2 * core)
+
+    pending = []
+
+    def finish():
+        for wait in pending:
+            wait()
+
+    def when_done(condition, waits):
+        def wait_all():
+            @pl.when(condition)
+            def _():
+                for wait in waits:
+                    wait()
+
+        pending.append(wait_all)
+
+    barrier = pltpu.get_barrier_semaphore()
+
+    def greet(device):
+        pl.semaphore_signal(barrier, inc=1, device_id=device, device_id_type=MESH)
+
+    @pl.when(has_next)
+    def _():
+        greet((base + GROUP, t))
+        greet((base + GROUP + 1, t))
+
+    @pl.when(follows)
+    def _():
+        for e in range(GROUP):
+            greet((base - GROUP + e, t))
+
+    for off in range(1, GROUP):
+        greet((base + (m + off) % GROUP, t))
+    greet(partner)
+    for off in range(1, chips):
+        greet((s, ((chip + off) % chips) * 2 + core))
 
     step = width // W_CHUNKS
     loads = []
@@ -62,39 +101,21 @@
         ])
     q_load = pltpu.make_async_copy(q_hbm, q_v, load_sem.at[3 * W_CHUNKS])
     do_load = pltpu.make_async_copy(do_hbm, do_v, load_sem.at[3 * W_CHUNKS + 1])
+    small_loads = [
+        pltpu.make_async_copy(src, dst, small_sem.at[i])
+        for i, (src, dst) in enumerate([
+            (kg_hbm, kg_ref), (qg_hbm, qg_ref), (slot_hbm, slot_ref), (tiles_hbm, tiles_ref),
+            (range_hbm, range_ref),
+        ])
+    ]
+    small_loads[0].start()
     for group_loads in loads:
         for copy in group_loads:
             copy.start()
     q_load.start()
     do_load.start()
-
-    barrier = pltpu.get_barrier_semaphore()
-
-    def greet(device):
-        pl.semaphore_signal(barrier, inc=1, device_id=device, device_id_type=MESH)
-
-    for off in range(1, GROUP):
-        greet((base + (m + off) % GROUP, t))
-    greet(partner)
-    for off in range(1, chips):
-        greet((s, ((chip + off) % chips) * 2 + core))
-
-    @pl.when(has_next)
-    def _():
-        greet((base + GROUP, t))
-
-    @pl.when(has_next & (m == GROUP - 1))
-    def _():
-        greet((base + GROUP + 1, t))
-
-    @pl.when(has_prev & (m == 0))
-    def _():
-        for e in range(GROUP):
-            greet((base - GROUP + e, t))
-
-    @pl.when(has_prev & (m == 1))
-    def _():
-        greet((base - 1, t))
+    for copy in small_loads[1:]:
+        copy.start()
 
     acc = jnp.zeros((rows, 2 * head), F32)
     for i in range(W_CHUNKS):
@@ -102,6 +123,7 @@
             copy.wait()
         part = slice(i * step, (i + 1) * step)
         acc = acc + dot(f_v[:, part], w_v[part, :], ((1,), (0,)))
+    small_loads[0].wait()
     raw = acc[:, :head]
     raw_v[...] = raw
     kinv = lax.rsqrt(jnp.mean(raw * raw, axis=-1, keepdims=True) + 1e-05)
@@ -110,10 +132,8 @@
 
     peers = (
         GROUP - 1 + chips
-        + jnp.where(has_next, 1, 0)
-        + jnp.where(has_next & (m == GROUP - 1), 1, 0)
-        + jnp.where(has_prev & (m == 0), GROUP, 0)
-        + jnp.where(has_prev & (m == 1), 1, 0)
+        + jnp.where(has_next, 2, 0)
+        + jnp.where(follows, GROUP, 0)
     )
     pl.semaphore_wait(barrier, peers)
 
@@ -123,10 +143,10 @@
             device_id=device, device_id_type=MESH,
         )
 
-    def kv_cross():
+    def kv_cross(i):
         return remote(
-            kv_in.at[m], kv_in.at[GROUP + m], kv_send.at[GROUP - 1], kv_recv.at[GROUP + m],
-            (base + GROUP, t),
+            kv_in.at[m], kv_in.at[GROUP + m], kv_send.at[GROUP - 1 + i], kv_recv.at[GROUP + m],
+            (base + GROUP + i, t),
         )
 
     def kv_group(off):
@@ -140,12 +160,18 @@
 
     @pl.when(has_next)
     def _():
-        kv_cross().start()
+        for i in range(2):
+            kv_cross(i).start()
+
+    when_done(has_next, [lambda i=i: kv_cross(i).wait_send() for i in range(2)])
 
     for off in range(1, GROUP):
         kv_group(off).start()
+        pending.append(lambda off=off: kv_group(off).wait_send())
 
     q_load.wait()
+    for copy in small_loads[1:]:
+        copy.wait()
     for h in range(heads):
         cols = slice(h * head, (h + 1) * head)
         x = q_v[:, cols].astype(F32)
@@ -155,7 +181,7 @@
         q16_v[:, cols] = normed
         qt_v[h] = normed.astype(F32).T.astype(BF16)
 
-    blocks = range_ref.shape[0]
+    blocks = range_ref.shape[1]
     per_block = toks // blocks
     block_of = lax.broadcasted_iota(jnp.int32, (1, toks), 1) // per_block
     row_of = lax.broadcasted_iota(jnp.int32, (rows, toks), 0)
@@ -164,7 +190,7 @@
         live = tiles_ref[jnp.maximum(image, 0)] * TILE_ROWS
         limit = jnp.zeros((1, toks), jnp.int32)
         for b in range(blocks):
-            seen = (range_ref[b, 0] <= image) & (image < range_ref[b, 1])
+            seen = (range_ref[0, b] <= image) & (image < range_ref[1, b])
             limit = jnp.where(block_of == b, jnp.where(seen, live, 0), limit)
         bias_v[j * rows:(j + 1) * rows, :] = jnp.where(row_of < limit, 0.0, HIDDEN)
     do_load.wait()
@@ -179,32 +205,16 @@
             chosen = jnp.where(ids[e] == image, kv_in[e], chosen)
         kcat[j * rows:(j + 1) * rows, :] = chosen
 
-    last = pl.ds((LOOKBACK - 1) * rows, rows)
-
-    def kv_relay():
-        return remote(
-            kcat.at[last], kv_in.at[GROUP], relay_sem, kv_recv.at[GROUP], (base + GROUP + 1, t)
-        )
-
-    @pl.when(has_next & (m == GROUP - 1))
-    def _():
-        kv_relay().start()
-
-    @pl.when(has_prev & (m == 0))
+    @pl.when(follows)
     def _():
         for e in range(GROUP):
             kv_arrived(GROUP + e)
         for j in range(LOOKBACK - 1):
             image = s - (LOOKBACK - 1) + j
-            chosen = jnp.zeros((rows, 2 * head), BF16)
+            chosen = kcat[j * rows:(j + 1) * rows, :]
             for e in range(GROUP):
                 chosen = jnp.where(slot_ref[base - GROUP + e] == image, kv_in[GROUP + e], chosen)
             kcat[j * rows:(j + 1) * rows, :] = chosen
-
-    @pl.when(has_prev & (m == 1))
-    def _():
-        kv_arrived(GROUP)
-        kcat[:rows, :] = kv_in[GROUP]
 
     keys = kcat[:, :head]
     values = kcat[:, head:]
@@ -219,7 +229,7 @@
         delta = jnp.sum(p * dp, axis=0, keepdims=True)
         ds_v[h] = (p * (dp - delta)).astype(BF16)
 
-    for j in range(LOOKBACK):
+    def image_grads(j):
         part = slice(j * rows, (j + 1) * rows)
         dk = jnp.zeros((rows, head), F32)
         dv = jnp.zeros((rows, head), F32)
@@ -236,27 +246,20 @@
             total = jnp.where(image_id == s - (LOOKBACK - 1) + j, g_v[j], total)
         return total
 
+    for j in range(LOOKBACK - 1):
+        image_grads(j)
+
     def cross_back(e):
-        return remote(csend.at[e], crecv, c_send.at[e], c_recv, (base - GROUP + e, t))
-
-    def relay_back():
-        return remote(csend.at[0], rrecv, rg_send, rg_recv, (base - 1, t))
-
-    @pl.when(has_prev & (m == 0))
+        return remote(csend.at[e], crecv.at[m], c_send.at[e], c_recv.at[m], (base - GROUP + e, t))
+
+    @pl.when(follows)
     def _():
         for e in range(GROUP):
             csend[e] = for_slot(slot_ref[base - GROUP + e], LOOKBACK - 1).astype(BF16)
             cross_back(e).start()
 
-    @pl.when(has_prev & (m == 1))
-    def _():
-        csend[0] = g_v[0].astype(BF16)
-        relay_back().start()
-
-    @pl.when(has_next & (m == GROUP - 1))
-    def _():
-        pltpu.make_async_copy(rrecv, rrecv, rg_recv).wait()
-        g_v[LOOKBACK - 1] = g_v[LOOKBACK - 1] + rrecv[...].astype(F32)
+    when_done(follows, [lambda e=e: cross_back(e).wait_send() for e in range(GROUP)])
+    image_grads(LOOKBACK - 1)
 
     def group_back(off):
         return remote(
@@ -267,6 +270,7 @@
     for off in range(1, GROUP):
         gsend[off - 1] = for_slot(slot_ref[base + (m + off) % GROUP], LOOKBACK).astype(BF16)
         group_back(off).start()
+        pending.append(lambda off=off: group_back(off).wait_send())
 
     for h in range(heads):
         cols = slice(h * head, (h + 1) * head)
@@ -280,6 +284,7 @@
     gq_store = pltpu.make_async_copy(gq_v, gq_hbm, store_sem.at[1])
     att_store.start()
     gq_store.start()
+    pending.extend([att_store.wait, gq_store.wait])
 
     mine = for_slot(slot_ref[s], LOOKBACK)
     g_v[0] = mine
@@ -289,8 +294,9 @@
 
     @pl.when(has_next)
     def _():
-        pltpu.make_async_copy(crecv, crecv, c_recv).wait()
-        g_v[0] = g_v[0] + crecv[...].astype(F32)
+        for i in range(2):
+            pltpu.make_async_copy(crecv.at[i], crecv.at[i], c_recv.at[i]).wait()
+            g_v[0] = g_v[0] + crecv[i].astype(F32)
 
     raw = raw_v[...]
     kinv = lax.rsqrt(jnp.mean(raw * raw, axis=-1, keepdims=True) + 1e-05)
@@ -308,58 +314,59 @@
     def to_partner(i):
         return remote(psend.at[i], precv.at[i], p_send.at[i], p_recv.at[i], partner)
 
+    mate = chip + (1 - 2 * (chip % 2))
+    far_mate = chips - 1 - mate
+    far_same = chips - 1 - chip
+    order = [
+        inner * far_same + (1 - inner) * far_same,
+        inner * mate + (1 - inner) * far_mate,
+        inner * far_mate + (1 - inner) * mate,
+        chip,
+    ]
+    target = [inner * order[0] + (1 - inner) * mate, order[1], order[2]]
+    landing = [3 - 2 * inner, 2 - 2 * inner, inner]
+
     def to_chip(i):
         return remote(
-            bsend.at[i - 1], brecv.at[i - 1], b_send.at[i - 1], b_recv.at[i - 1],
-            (s, ((chip + i) % chips) * 2 + core),
+            bsend.at[i], brecv.at[landing[i]], b_send.at[i], b_recv.at[landing[i]],
+            (s, target[i] * 2 + core),
         )
 
-    order = list(range(1, chips)) + [0]
-    for i in order:
-        psend[i] = term(((chip + i) % chips) * 2 + 1 - core).astype(BF16)
+    def landed(slot):
+        pltpu.make_async_copy(brecv.at[slot], brecv.at[slot], b_recv.at[slot]).wait()
+        return brecv[slot].astype(F32)
+
+    for i in range(chips):
+        psend[i] = term(order[i] * 2 + 1 - core).astype(BF16)
         to_partner(i).start()
-    for i in order:
-        own = term(((chip + i) % chips) * 2 + core).astype(BF16).astype(F32)
+        pending.append(lambda i=i: to_partner(i).wait_send())
+    for i in (0, 1, 3, 2):
+        own = term(order[i] * 2 + core).astype(BF16).astype(F32)
         to_partner(i).wait_recv()
         both = own + precv[i].astype(F32)
-        if i:
-            bsend[i - 1] = both.astype(BF16)
-            to_chip(i).start()
-    for i in range(1, chips):
-        to_chip(i).wait_recv()
-        both = both + brecv[i - 1].astype(F32)
+        if i == 3:
+            sum_v[...] = both
+            continue
+        bsend[i] = both.astype(BF16)
+        if i == 2:
+            @pl.when(inner == 1)
+            def _():
+                bsend[2] = (bsend[2].astype(F32) + landed(3)).astype(BF16)
+        to_chip(i).start()
+        pending.append(lambda i=i: to_chip(i).wait_send())
+    sum_v[...] = sum_v[...] + landed(0)
+
+    @pl.when(inner == 1)
+    def _():
+        sum_v[...] = sum_v[...] + landed(2)
+
+    both = sum_v[...] + landed(1)
     gf_v[...] = both.astype(BF16)
     gf_store = pltpu.make_async_copy(gf_v, gf_hbm, store_sem.at[2])
     gf_store.start()
-
-    for off in range(1, GROUP):
-        kv_group(off).wait_send()
-        group_back(off).wait_send()
-
-    @pl.when(has_next)
-    def _():
-        kv_cross().wait_send()
-
-    @pl.when(has_next & (m == GROUP - 1))
-    def _():
-        kv_relay().wait_send()
-
-    @pl.when(has_prev & (m == 0))
-    def _():
-        for e in range(GROUP):
-            cross_back(e).wait_send()
-
-    @pl.when(has_prev & (m == 1))
-    def _():
-        relay_back().wait_send()
-
-    for i in range(chips):
-        to_partner(i).wait_send()
-    for i in range(1, chips):
-        to_chip(i).wait_send()
-    att_store.wait()
-    gq_store.wait()
-    gf_store.wait()
+    pending.append(gf_store.wait)
+
+    finish()
 
 
 def local(
@@ -376,9 +383,13 @@
     out_cols = width // tensor_count
     dma = pltpu.SemaphoreType.DMA
     any_space = pl.BlockSpec(memory_space=pl.ANY)
-    vmem = pl.BlockSpec(memory_space=pltpu.VMEM)
-    smem = pl.BlockSpec(memory_space=pltpu.SMEM)
+    hbm = pl.BlockSpec(memory_space=pltpu.HBM)
     scratch = [
+        pltpu.VMEM((1, head), F32),
+        pltpu.VMEM((1, head), F32),
+        pltpu.SMEM(slot_image.shape, jnp.int32),
+        pltpu.SMEM(image_tiles.shape, jnp.int32),
+        pltpu.SMEM(image_range.shape[::-1], jnp.int32),
         pltpu.VMEM((rows, width), BF16),
         pltpu.VMEM((width, 2 * head), BF16),
         pltpu.VMEM((toks, q_cols), BF16),
@@ -399,28 +410,26 @@
         pltpu.VMEM((GROUP - 1, rows, 2 * head), BF16),
         pltpu.VMEM((GROUP - 1, rows, 2 * head), BF16),
         pltpu.VMEM((GROUP, rows, 2 * head), BF16),
-        pltpu.VMEM((rows, 2 * head), BF16),
-        pltpu.VMEM((rows, 2 * head), BF16),
+        pltpu.VMEM((2, rows, 2 * head), BF16),
         pltpu.VMEM((rows, 2 * head), BF16),
         pltpu.VMEM((chips, rows, out_cols), BF16),
         pltpu.VMEM((chips, rows, out_cols), BF16),
         pltpu.VMEM((chips - 1, rows, out_cols), BF16),
-        pltpu.VMEM((chips - 1, rows, out_cols), BF16),
+        pltpu.VMEM((chips, rows, out_cols), BF16),
+        pltpu.VMEM((rows, out_cols), F32),
+        dma((5,)),
         dma((3 * W_CHUNKS + 2,)),
         dma((3,)),
-        dma((GROUP,)),
+        dma((GROUP + 1,)),
         dma((2 * GROUP,)),
-        dma,
         dma((GROUP - 1,)),
         dma((GROUP - 1,)),
         dma((GROUP,)),
-        dma,
-        dma,
-        dma,
+        dma((2,)),
         dma((chips,)),
         dma((chips,)),
         dma((chips - 1,)),
-        dma((chips - 1,)),
+        dma((chips,)),
     ]
     return pl.pallas_call(
         functools.partial(kernel, seq_count, tensor_count),
@@ -429,18 +438,18 @@
             jax.ShapeDtypeStruct((toks, q_cols), BF16),
             jax.ShapeDtypeStruct((rows, out_cols), BF16),
         ),
-        in_specs=[any_space] * 4 + [vmem] * 2 + [smem] * 3 + [any_space],
+        in_specs=[hbm] * 10,
         out_specs=(any_space,) * 3,
         scratch_shapes=scratch,
         compiler_params=pltpu.CompilerParams(
-            collective_id=0, has_side_effects=True, vmem_limit_bytes=48 * 1024 * 1024
+            collective_id=0, has_side_effects=True, vmem_limit_bytes=105 * 512 * 1024
         ),
         cost_estimate=pl.CostEstimate(
             flops=1_300_000_000, bytes_accessed=5_500_000, transcendentals=600_000
         ),
     )(
         queries, features, w_key, w_value, q_gain.reshape(1, head), k_gain.reshape(1, head),
-        slot_image, image_tiles, image_range, d_out,
+        slot_image, image_tiles, image_range.T, d_out,
     )
 
 

time: 61.6 us -> 48.2 us (0.78)
  the two profiles are of different devices: /device:TPU:15 before, /device:TPU:441 now
where the time goes in v2:
time: 48.2 us; the launch traced here: 48.1 us
  Pallas kernels  44.5 us (92%)
  local copies, waits for them, and re-layouts  2.92 us (6%)
  between operations  0.69 us (1%)
    pallas_call x1, Pallas kernels, local(): pl.pallas_call(functools.partial(kernel, seq_count, tensor_count), out_sh...  44.5 us
    unnamed x13, local copies, waits for them, and re-layouts  2.92 us

profile of v2, /device:TPU:441, one launch (start us, length us, event | category | flops | bytes accessed | tf_op | source)
XLA Modules:
  0.0 48.1 jit_solution(9791915580423287871)
XLA Ops:
  0.6 0.0 copy-start.2
  0.6 0.0 copy-start.3
  0.7 0.0 copy-start.4
  0.7 0.0 copy-start
  0.7 0.0 copy-start.1
  0.7 0.6 %copy-done.2 = f32[128]{0:T(128)S(1)} copy-done((f32[128]{0:T(128)S(1)}, f32[128]{0:T(128)}, u32[]{:S(2)}) %copy-start.2) | copy-done | bytes 536
  1.3 0.0 copy-done.3
  1.3 0.0 copy-done.4
  1.3 0.0 copy-done
  1.4 0.0 copy-done.1
  1.4 44.5 %shard_map.121 = (bf16[256,1024]{1,0:T(8,128)(2,1)S(1)}, bf16[256,1024]{1,0:T(8,128)(2,1)S(1)}, bf16[96,512]{1,0:T(8,128)(2,1)S(1)}) custom-call(bf16[256,1024]{1,0:T(8,128)(2,1)} %q_hbm.1, bf16[96,4096]{1,0:T(8,128)(2,1)} %f_hbm.1, bf16[4096,128]{1,0:T(8,128)(2,1)} %wk_hbm.1, bf16[4096,128]{1,0:T(8,128)(2,1)} %wv_hbm.1, f32[1,128]{1,0:T(1,128)S(1)} %bitcast.4, ...), custom_call_target="tpu_custom_call" | custom-call | flops 1300000000 | bytes 5500000 | tf_op jit(solution)/shard_map/pallas_call | solution.py:434
  45.9 0.8 %copy.16 = bf16[256,1024]{1,0:T(8,128)(2,1)} copy(bf16[256,1024]{1,0:T(8,128)(2,1)S(1)} %get-tuple-element.6) | data formatting | bytes 1048576
  46.7 0.8 %copy.17 = bf16[256,1024]{1,0:T(8,128)(2,1)} copy(bf16[256,1024]{1,0:T(8,128)(2,1)S(1)} %get-tuple-element.7) | data formatting | bytes 1048576
  47.5 0.6 %copy.18 = bf16[96,512]{1,0:T(8,128)(2,1)} copy(bf16[96,512]{1,0:T(8,128)(2,1)S(1)} %get-tuple-element.8) | data formatting | bytes 196608
Async XLA Ops:
  0.6 0.7 %copy-start.2 = (f32[128]{0:T(128)S(1)}, f32[128]{0:T(128)}, u32[]{:S(2)}) copy-start(f32[128]{0:T(128)} %param.15) | copy-start | bytes 1540
  0.6 0.7 %copy-start.3 = (s32[64]{0:T(128)S(1)}, s32[64]{0:T(128)}, u32[]{:S(2)}) copy-start(s32[64]{0:T(128)} %slot_hbm.1) | copy-start | bytes 772
  0.7 0.7 %copy-start.4 = (s32[64]{0:T(128)S(1)}, s32[64]{0:T(128)}, u32[]{:S(2)}) copy-start(s32[64]{0:T(128)} %tiles_hbm.1) | copy-start | bytes 772
  0.7 0.7 %copy-start = (s32[4,2]{0,1:T(2,128)S(1)}, s32[4,2]{0,1:T(2,128)}, u32[]{:S(2)}) copy-start(s32[4,2]{0,1:T(2,128)} %param.18) | copy-start | bytes 100
  0.7 0.7 %copy-start.1 = (f32[128]{0:T(128)S(1)}, f32[128]{0:T(128)}, u32[]{:S(2)}) copy-start(f32[128]{0:T(128)} %param.14) | copy-start | bytes 1540

commit v3 on v2

--- a/solution.py
+++ b/solution.py
@@ -50,7 +50,6 @@
     scale = head ** (-0.5)
     has_next = g < groups - 1
     has_prev = g > 0
-    follows = has_prev & (m < 2)
     inner = (chip % 3 + 1) // 2
     partner = (s, t + 1 - 2 * core)
 
@@ -79,7 +78,7 @@
         greet((base + GROUP, t))
         greet((base + GROUP + 1, t))
 
-    @pl.when(follows)
+    @pl.when(has_prev & (m < 2))
     def _():
         for e in range(GROUP):
             greet((base - GROUP + e, t))
@@ -133,7 +132,7 @@
     peers = (
         GROUP - 1 + chips
         + jnp.where(has_next, 2, 0)
-        + jnp.where(follows, GROUP, 0)
+        + jnp.where(has_prev & (m < 2), GROUP, 0)
     )
     pl.semaphore_wait(barrier, peers)
 
@@ -143,10 +142,10 @@
             device_id=device, device_id_type=MESH,
         )
 
-    def kv_cross(i):
+    def kv_cross():
         return remote(
-            kv_in.at[m], kv_in.at[GROUP + m], kv_send.at[GROUP - 1 + i], kv_recv.at[GROUP + m],
-            (base + GROUP + i, t),
+            kv_in.at[m], kv_in.at[GROUP + m], kv_send.at[GROUP - 1], kv_recv.at[GROUP + m],
+            (base + GROUP, t),
         )
 
     def kv_group(off):
@@ -160,10 +159,9 @@
 
     @pl.when(has_next)
     def _():
-        for i in range(2):
-            kv_cross(i).start()
-
-    when_done(has_next, [lambda i=i: kv_cross(i).wait_send() for i in range(2)])
+        kv_cross().start()
+
+    when_done(has_next, [lambda: kv_cross().wait_send()])
 
     for off in range(1, GROUP):
         kv_group(off).start()
@@ -205,16 +203,31 @@
             chosen = jnp.where(ids[e] == image, kv_in[e], chosen)
         kcat[j * rows:(j + 1) * rows, :] = chosen
 
-    @pl.when(follows)
+    def kv_relay():
+        return remote(
+            kcat.at[pl.ds(rows, rows)], kv_in.at[GROUP], kv_send.at[GROUP], kv_recv.at[GROUP],
+            (s + 1, t),
+        )
+
+    @pl.when(has_prev & (m == 0))
     def _():
         for e in range(GROUP):
             kv_arrived(GROUP + e)
-        for j in range(LOOKBACK - 1):
+        for j in reversed(range(LOOKBACK - 1)):
             image = s - (LOOKBACK - 1) + j
             chosen = kcat[j * rows:(j + 1) * rows, :]
             for e in range(GROUP):
                 chosen = jnp.where(slot_ref[base - GROUP + e] == image, kv_in[GROUP + e], chosen)
             kcat[j * rows:(j + 1) * rows, :] = chosen
+            if j == 1:
+                kv_relay().start()
+
+    when_done(has_prev & (m == 0), [lambda: kv_relay().wait_send()])
+
+    @pl.when(has_prev & (m == 1))
+    def _():
+        kv_arrived(GROUP)
+        kcat[:rows, :] = kv_in[GROUP]
 
     keys = kcat[:, :head]
     values = kcat[:, head:]
@@ -246,20 +259,28 @@
             total = jnp.where(image_id == s - (LOOKBACK - 1) + j, g_v[j], total)
         return total
 
-    for j in range(LOOKBACK - 1):
-        image_grads(j)
-
     def cross_back(e):
         return remote(csend.at[e], crecv.at[m], c_send.at[e], c_recv.at[m], (base - GROUP + e, t))
 
-    @pl.when(follows)
-    def _():
-        for e in range(GROUP):
-            csend[e] = for_slot(slot_ref[base - GROUP + e], LOOKBACK - 1).astype(BF16)
-            cross_back(e).start()
-
-    when_done(follows, [lambda e=e: cross_back(e).wait_send() for e in range(GROUP)])
-    image_grads(LOOKBACK - 1)
+    def send_cross_back(count):
+        def send():
+            grads = [g_v[j].astype(BF16) for j in range(count)]
+            for e in range(GROUP):
+                chosen = jnp.zeros((rows, 2 * head), BF16)
+                for j in range(count):
+                    image = s - (LOOKBACK - 1) + j
+                    chosen = jnp.where(slot_ref[base - GROUP + e] == image, grads[j], chosen)
+                csend[e] = chosen
+                cross_back(e).start()
+
+        return send
+
+    image_grads(0)
+    pl.when(has_prev & (m == 1))(send_cross_back(1))
+    image_grads(1)
+    pl.when(has_prev & (m == 0))(send_cross_back(2))
+    when_done(has_prev & (m < 2), [lambda e=e: cross_back(e).wait_send() for e in range(GROUP)])
+    image_grads(2)
 
     def group_back(off):
         return remote(
@@ -286,8 +307,11 @@
     gq_store.start()
     pending.extend([att_store.wait, gq_store.wait])
 
-    mine = for_slot(slot_ref[s], LOOKBACK)
-    g_v[0] = mine
+    def arrived(buffer, sem, slot):
+        pltpu.make_async_copy(buffer.at[slot], buffer.at[slot], sem.at[slot]).wait()
+        return buffer[slot].astype(F32)
+
+    g_v[0] = for_slot(slot_ref[s], LOOKBACK)
     for off in range(1, GROUP):
         group_back(off).wait_recv()
         g_v[0] = g_v[0] + grecv[off - 1].astype(F32)
@@ -295,8 +319,7 @@
     @pl.when(has_next)
     def _():
         for i in range(2):
-            pltpu.make_async_copy(crecv.at[i], crecv.at[i], c_recv.at[i]).wait()
-            g_v[0] = g_v[0] + crecv[i].astype(F32)
+            g_v[0] = g_v[0] + arrived(crecv, c_recv, i)
 
     raw = raw_v[...]
     kinv = lax.rsqrt(jnp.mean(raw * raw, axis=-1, keepdims=True) + 1e-05)

time: 48.2 us -> 47.1 us (0.977)
  the two profiles are of different devices: /device:TPU:441 before, /device:TPU:7 now
where the time goes in v3:
time: 47.1 us; the launch traced here: 46.8 us
  Pallas kernels  43.2 us (92%)
  local copies, waits for them, and re-layouts  2.92 us (6%)
  between operations  0.69 us (1%)
    pallas_call x1, Pallas kernels, local(): pl.pallas_call(functools.partial(kernel, seq_count, tensor_count), out_sh...  43.2 us
    unnamed x13, local copies, waits for them, and re-layouts  2.92 us

profile of v3, /device:TPU:7, one launch (start us, length us, event | category | flops | bytes accessed | tf_op | source)
XLA Modules:
  0.0 46.8 jit_solution(7025988414689724926)
XLA Ops:
  0.6 0.0 copy-start.2
  0.6 0.0 copy-start.3
  0.7 0.0 copy-start.4
  0.7 0.0 copy-start
  0.7 0.0 copy-start.1
  0.7 0.6 %copy-done.2 = f32[128]{0:T(128)S(1)} copy-done((f32[128]{0:T(128)S(1)}, f32[128]{0:T(128)}, u32[]{:S(2)}) %copy-start.2) | copy-done | bytes 536
  1.3 0.0 copy-done.3
  1.3 0.0 copy-done.4
  1.3 0.0 copy-done
  1.4 0.0 copy-done.1
  1.4 43.2 %shard_map.121 = (bf16[256,1024]{1,0:T(8,128)(2,1)S(1)}, bf16[256,1024]{1,0:T(8,128)(2,1)S(1)}, bf16[96,512]{1,0:T(8,128)(2,1)S(1)}) custom-call(bf16[256,1024]{1,0:T(8,128)(2,1)} %q_hbm.1, bf16[96,4096]{1,0:T(8,128)(2,1)} %f_hbm.1, bf16[4096,128]{1,0:T(8,128)(2,1)} %wk_hbm.1, bf16[4096,128]{1,0:T(8,128)(2,1)} %wv_hbm.1, f32[1,128]{1,0:T(1,128)S(1)} %bitcast.4, ...), custom_call_target="tpu_custom_call" | custom-call | flops 1300000000 | bytes 5500000 | tf_op jit(solution)/shard_map/pallas_call | solution.py:457
  44.6 0.8 %copy.16 = bf16[256,1024]{1,0:T(8,128)(2,1)} copy(bf16[256,1024]{1,0:T(8,128)(2,1)S(1)} %get-tuple-element.6) | data formatting | bytes 1048576
  45.3 0.8 %copy.17 = bf16[256,1024]{1,0:T(8,128)(2,1)} copy(bf16[256,1024]{1,0:T(8,128)(2,1)S(1)} %get-tuple-element.7) | data formatting | bytes 1048576
  46.1 0.6 %copy.18 = bf16[96,512]{1,0:T(8,128)(2,1)} copy(bf16[96,512]{1,0:T(8,128)(2,1)S(1)} %get-tuple-element.8) | data formatting | bytes 196608
Async XLA Ops:
  0.6 0.7 %copy-start.2 = (f32[128]{0:T(128)S(1)}, f32[128]{0:T(128)}, u32[]{:S(2)}) copy-start(f32[128]{0:T(128)} %param.15) | copy-start | bytes 1540
  0.6 0.7 %copy-start.3 = (s32[64]{0:T(128)S(1)}, s32[64]{0:T(128)}, u32[]{:S(2)}) copy-start(s32[64]{0:T(128)} %slot_hbm.1) | copy-start | bytes 772
  0.7 0.7 %copy-start.4 = (s32[64]{0:T(128)S(1)}, s32[64]{0:T(128)}, u32[]{:S(2)}) copy-start(s32[64]{0:T(128)} %tiles_hbm.1) | copy-start | bytes 772
  0.7 0.7 %copy-start = (s32[4,2]{0,1:T(2,128)S(1)}, s32[4,2]{0,1:T(2,128)}, u32[]{:S(2)}) copy-start(s32[4,2]{0,1:T(2,128)} %param.18) | copy-start | bytes 100
  0.7 0.7 %copy-start.1 = (f32[128]{0:T(128)S(1)}, f32[128]{0:T(128)}, u32[]{:S(2)}) copy-start(f32[128]{0:T(128)} %param.14) | copy-start | bytes 1540

commit v4 on v3

--- a/solution.py
+++ b/solution.py
@@ -28,7 +28,7 @@
     att_hbm, gq_hbm, gf_hbm,
     qg_ref, kg_ref, slot_ref, tiles_ref, range_ref,
     f_v, w_v, q_v, do_v, att_v, gq_v, gf_v,
-    raw_v, kv_in, kcat, q16_v, qt_v, inv_v, bias_v, p_v, ds_v,
+    raw_v, kv_in, kcat, e_v, dp_v, total_v, weighted_v, q16_v, qt_v, inv_v, bias_v, p_v, ds_v,
     g_v, gsend, grecv, csend, crecv, a_v,
     psend, precv, bsend, brecv, sum_v,
     small_sem, load_sem, store_sem, kv_send, kv_recv, g_send, g_recv, c_send, c_recv,
@@ -73,6 +73,9 @@
     def greet(device):
         pl.semaphore_signal(barrier, inc=1, device_id=device, device_id_type=MESH)
 
+    for off in range(1, GROUP):
+        greet((base + (m + off) % GROUP, t))
+
     @pl.when(has_next)
     def _():
         greet((base + GROUP, t))
@@ -83,8 +86,6 @@
         for e in range(GROUP):
             greet((base - GROUP + e, t))
 
-    for off in range(1, GROUP):
-        greet((base + (m + off) % GROUP, t))
     greet(partner)
     for off in range(1, chips):
         greet((s, ((chip + off) % chips) * 2 + core))
@@ -111,8 +112,6 @@
     for group_loads in loads:
         for copy in group_loads:
             copy.start()
-    q_load.start()
-    do_load.start()
     for copy in small_loads[1:]:
         copy.start()
 
@@ -122,6 +121,8 @@
             copy.wait()
         part = slice(i * step, (i + 1) * step)
         acc = acc + dot(f_v[:, part], w_v[part, :], ((1,), (0,)))
+    q_load.start()
+    do_load.start()
     small_loads[0].wait()
     raw = acc[:, :head]
     raw_v[...] = raw
@@ -203,6 +204,34 @@
             chosen = jnp.where(ids[e] == image, kv_in[e], chosen)
         kcat[j * rows:(j + 1) * rows, :] = chosen
 
+    def scan(low, high, first):
+        def some():
+            part = slice(low * rows, high * rows)
+            for h in range(heads):
+                cols = slice(h * head, (h + 1) * head)
+                scores = dot(kcat[part, :head], qt_v[h], ((1,), (0,)))
+                e = jnp.exp2(scores * (scale * LOG2E) + bias_v[part, :])
+                dp = dot(kcat[part, head:], do_v[:, cols], ((1,), (1,)))
+                e_v[h, part, :] = e
+                dp_v[h, part, :] = dp
+                total = jnp.sum(e, axis=0, keepdims=True)
+                weighted = jnp.sum(e * dp, axis=0, keepdims=True)
+                total_v[h] = total if first else total_v[h] + total
+                weighted_v[h] = weighted if first else weighted_v[h] + weighted
+
+        return some
+
+    def settle(j):
+        part = slice(j * rows, (j + 1) * rows)
+        for h in range(heads):
+            total = total_v[h]
+            inverse = jnp.where(total > 0.0, 1.0 / total, 0.0)
+            p = e_v[h, part, :] * inverse
+            p_v[h, part, :] = p.astype(BF16)
+            ds_v[h, part, :] = (p * (dp_v[h, part, :] - weighted_v[h] * inverse)).astype(BF16)
+
+    pl.when(m == 1)(scan(1, 3, True))
+
     def kv_relay():
         return remote(
             kcat.at[pl.ds(rows, rows)], kv_in.at[GROUP], kv_send.at[GROUP], kv_recv.at[GROUP],
@@ -229,18 +258,20 @@
         kv_arrived(GROUP)
         kcat[:rows, :] = kv_in[GROUP]
 
-    keys = kcat[:, :head]
-    values = kcat[:, head:]
-    for h in range(heads):
-        cols = slice(h * head, (h + 1) * head)
-        scores = dot(keys, qt_v[h], ((1,), (0,)))
-        e = jnp.exp2(scores * (scale * LOG2E) + bias_v[...])
-        total = jnp.sum(e, axis=0, keepdims=True)
-        p = e * jnp.where(total > 0.0, 1.0 / total, 0.0)
-        p_v[h] = p.astype(BF16)
-        dp = dot(values, do_v[:, cols], ((1,), (1,)))
-        delta = jnp.sum(p * dp, axis=0, keepdims=True)
-        ds_v[h] = (p * (dp - delta)).astype(BF16)
+    pl.when(m == 1)(scan(0, 1, False))
+
+    @pl.when(m != 1)
+    def _():
+        for h in range(heads):
+            cols = slice(h * head, (h + 1) * head)
+            scores = dot(kcat[:, :head], qt_v[h], ((1,), (0,)))
+            e = jnp.exp2(scores * (scale * LOG2E) + bias_v[...])
+            total = jnp.sum(e, axis=0, keepdims=True)
+            p = e * jnp.where(total > 0.0, 1.0 / total, 0.0)
+            p_v[h] = p.astype(BF16)
+            dp = dot(kcat[:, head:], do_v[:, cols], ((1,), (1,)))
+            delta = jnp.sum(p * dp, axis=0, keepdims=True)
+            ds_v[h] = (p * (dp - delta)).astype(BF16)
 
     def image_grads(j):
         part = slice(j * rows, (j + 1) * rows)
@@ -275,8 +306,15 @@
 
         return send
 
+    pl.when(m == 1)(lambda: settle(0))
     image_grads(0)
     pl.when(has_prev & (m == 1))(send_cross_back(1))
+
+    @pl.when(m == 1)
+    def _():
+        settle(1)
+        settle(2)
+
     image_grads(1)
     pl.when(has_prev & (m == 0))(send_cross_back(2))
     when_done(has_prev & (m < 2), [lambda e=e: cross_back(e).wait_send() for e in range(GROUP)])
@@ -293,6 +331,8 @@
         group_back(off).start()
         pending.append(lambda off=off: group_back(off).wait_send())
 
+    keys = kcat[:, :head]
+    values = kcat[:, head:]
     for h in range(heads):
         cols = slice(h * head, (h + 1) * head)
         att_v[:, cols] = dot(p_v[h], values, ((0,), (0,))).astype(BF16)
@@ -423,6 +463,10 @@
         pltpu.VMEM((rows, head), F32),
         pltpu.VMEM((2 * GROUP, rows, 2 * head), BF16),
         pltpu.VMEM((keys, 2 * head), BF16),
+        pltpu.VMEM((heads, keys, toks), F32),
+        pltpu.VMEM((heads, keys, toks), F32),
+        pltpu.VMEM((heads, 1, toks), F32),
+        pltpu.VMEM((heads, 1, toks), F32),
         pltpu.VMEM((toks, q_cols), BF16),
         pltpu.VMEM((heads, head, toks), BF16),
         pltpu.VMEM((heads, toks, head), F32),

time: 47.1 us -> 47 us (level)
  no operation moved by 1% of the time
where the time goes in v4:
time: 47 us; the launch traced here: 46.8 us
  Pallas kernels  43.2 us (92%)
  local copies, waits for them, and re-layouts  2.92 us (6%)
  between operations  0.69 us (1%)
    pallas_call x1, Pallas kernels, local(): pl.pallas_call(functools.partial(kernel, seq_count, tensor_count), out_sh...  43.2 us
    unnamed x13, local copies, waits for them, and re-layouts  2.92 us

profile of v4, /device:TPU:7, one launch (start us, length us, event | category | flops | bytes accessed | tf_op | source)
XLA Modules:
  0.0 46.8 jit_solution(12046506500250802053)
XLA Ops:
  0.6 0.0 copy-start.2
  0.6 0.0 copy-start.3
  0.7 0.0 copy-start.4
  0.7 0.0 copy-start
  0.7 0.0 copy-start.1
  0.7 0.6 %copy-done.2 = f32[128]{0:T(128)S(1)} copy-done((f32[128]{0:T(128)S(1)}, f32[128]{0:T(128)}, u32[]{:S(2)}) %copy-start.2) | copy-done | bytes 536
  1.3 0.0 copy-done.3
  1.3 0.0 copy-done.4
  1.3 0.0 copy-done
  1.4 0.0 copy-done.1
  1.4 43.2 %shard_map.121 = (bf16[256,1024]{1,0:T(8,128)(2,1)S(1)}, bf16[256,1024]{1,0:T(8,128)(2,1)S(1)}, bf16[96,512]{1,0:T(8,128)(2,1)S(1)}) custom-call(bf16[256,1024]{1,0:T(8,128)(2,1)} %q_hbm.1, bf16[96,4096]{1,0:T(8,128)(2,1)} %f_hbm.1, bf16[4096,128]{1,0:T(8,128)(2,1)} %wk_hbm.1, bf16[4096,128]{1,0:T(8,128)(2,1)} %wv_hbm.1, f32[1,128]{1,0:T(1,128)S(1)} %bitcast.4, ...), custom_call_target="tpu_custom_call" | custom-call | flops 1300000000 | bytes 5500000 | tf_op jit(solution)/shard_map/pallas_call | solution.py:501
  44.6 0.8 %copy.16 = bf16[256,1024]{1,0:T(8,128)(2,1)} copy(bf16[256,1024]{1,0:T(8,128)(2,1)S(1)} %get-tuple-element.6) | data formatting | bytes 1048576
  45.4 0.8 %copy.17 = bf16[256,1024]{1,0:T(8,128)(2,1)} copy(bf16[256,1024]{1,0:T(8,128)(2,1)S(1)} %get-tuple-element.7) | data formatting | bytes 1048576
  46.2 0.6 %copy.18 = bf16[96,512]{1,0:T(8,128)(2,1)} copy(bf16[96,512]{1,0:T(8,128)(2,1)S(1)} %get-tuple-element.8) | data formatting | bytes 196608
Async XLA Ops:
  0.6 0.7 %copy-start.2 = (f32[128]{0:T(128)S(1)}, f32[128]{0:T(128)}, u32[]{:S(2)}) copy-start(f32[128]{0:T(128)} %param.15) | copy-start | bytes 1540
  0.6 0.7 %copy-start.3 = (s32[64]{0:T(128)S(1)}, s32[64]{0:T(128)}, u32[]{:S(2)}) copy-start(s32[64]{0:T(128)} %slot_hbm.1) | copy-start | bytes 772
  0.7 0.7 %copy-start.4 = (s32[64]{0:T(128)S(1)}, s32[64]{0:T(128)}, u32[]{:S(2)}) copy-start(s32[64]{0:T(128)} %tiles_hbm.1) | copy-start | bytes 772
  0.7 0.7 %copy-start = (s32[4,2]{0,1:T(2,128)S(1)}, s32[4,2]{0,1:T(2,128)}, u32[]{:S(2)}) copy-start(s32[4,2]{0,1:T(2,128)} %param.18) | copy-start | bytes 100
  0.7 0.7 %copy-start.1 = (f32[128]{0:T(128)S(1)}, f32[128]{0:T(128)}, u32[]{:S(2)}) copy-start(f32[128]{0:T(128)} %param.14) | copy-start | bytes 1540

commit v5 on v4

--- a/solution.py
+++ b/solution.py
@@ -143,10 +143,14 @@
             device_id=device, device_id_type=MESH,
         )
 
-    def kv_cross():
+    near_next = has_next & (g % 2 == 0)
+    near_prev = has_prev & (g % 2 == 1)
+    far_prev = has_prev & (g % 2 == 0)
+
+    def kv_cross(i):
         return remote(
-            kv_in.at[m], kv_in.at[GROUP + m], kv_send.at[GROUP - 1], kv_recv.at[GROUP + m],
-            (base + GROUP, t),
+            kv_in.at[m], kv_in.at[GROUP + m], kv_send.at[GROUP - 1 + 2 * i], kv_recv.at[GROUP + m],
+            (base + GROUP + i, t),
         )
 
     def kv_group(off):
@@ -160,9 +164,14 @@
 
     @pl.when(has_next)
     def _():
-        kv_cross().start()
-
-    when_done(has_next, [lambda: kv_cross().wait_send()])
+        kv_cross(0).start()
+
+    @pl.when(near_next)
+    def _():
+        kv_cross(1).start()
+
+    when_done(has_next, [lambda: kv_cross(0).wait_send()])
+    when_done(near_next, [lambda: kv_cross(1).wait_send()])
 
     for off in range(1, GROUP):
         kv_group(off).start()
@@ -249,14 +258,24 @@
                 chosen = jnp.where(slot_ref[base - GROUP + e] == image, kv_in[GROUP + e], chosen)
             kcat[j * rows:(j + 1) * rows, :] = chosen
             if j == 1:
-                kv_relay().start()
-
-    when_done(has_prev & (m == 0), [lambda: kv_relay().wait_send()])
-
-    @pl.when(has_prev & (m == 1))
+                pl.when(far_prev)(lambda: kv_relay().start())
+
+    when_done(far_prev & (m == 0), [lambda: kv_relay().wait_send()])
+
+    @pl.when(far_prev & (m == 1))
     def _():
         kv_arrived(GROUP)
         kcat[:rows, :] = kv_in[GROUP]
+
+    @pl.when(near_prev & (m == 1))
+    def _():
+        for e in range(GROUP):
+            kv_arrived(GROUP + e)
+        chosen = jnp.zeros((rows, 2 * head), BF16)
+        for e in range(GROUP):
+            held = slot_ref[base - GROUP + e] == s - (LOOKBACK - 1)
+            chosen = jnp.where(held, kv_in[GROUP + e], chosen)
+        kcat[:rows, :] = chosen
 
     pl.when(m == 1)(scan(0, 1, False))
 
@@ -487,7 +506,7 @@
         dma((5,)),
         dma((3 * W_CHUNKS + 2,)),
         dma((3,)),
-        dma((GROUP + 1,)),
+        dma((GROUP + 2,)),
         dma((2 * GROUP,)),
         dma((GROUP - 1,)),
         dma((GROUP - 1,)),

time: 47 us -> 47.3 us (level)
  no operation moved by 1% of the time
where the time goes in v5:
time: 47.3 us; the launch traced here: 47.1 us
  Pallas kernels  43.5 us (92%)
  local copies, waits for them, and re-layouts  2.92 us (6%)
  between operations  0.69 us (1%)
    pallas_call x1, Pallas kernels, local(): pl.pallas_call(functools.partial(kernel, seq_count, tensor_count), out_sh...  43.5 us
    unnamed x13, local copies, waits for them, and re-layouts  2.92 us

profile of v5, /device:TPU:7, one launch (start us, length us, event | category | flops | bytes accessed | tf_op | source)
XLA Modules:
  0.0 47.1 jit_solution(4176093678956376666)
XLA Ops:
  0.6 0.0 copy-start.2
  0.6 0.0 copy-start.3
  0.7 0.0 copy-start.4
  0.7 0.0 copy-start
  0.7 0.0 copy-start.1
  0.7 0.6 %copy-done.2 = f32[128]{0:T(128)S(1)} copy-done((f32[128]{0:T(128)S(1)}, f32[128]{0:T(128)}, u32[]{:S(2)}) %copy-start.2) | copy-done | bytes 536
  1.3 0.0 copy-done.3
  1.3 0.0 copy-done.4
  1.3 0.0 copy-done
  1.4 0.0 copy-done.1
  1.4 43.5 %shard_map.121 = (bf16[256,1024]{1,0:T(8,128)(2,1)S(1)}, bf16[256,1024]{1,0:T(8,128)(2,1)S(1)}, bf16[96,512]{1,0:T(8,128)(2,1)S(1)}) custom-call(bf16[256,1024]{1,0:T(8,128)(2,1)} %q_hbm.1, bf16[96,4096]{1,0:T(8,128)(2,1)} %f_hbm.1, bf16[4096,128]{1,0:T(8,128)(2,1)} %wk_hbm.1, bf16[4096,128]{1,0:T(8,128)(2,1)} %wv_hbm.1, f32[1,128]{1,0:T(1,128)S(1)} %bitcast.4, ...), custom_call_target="tpu_custom_call" | custom-call | flops 1300000000 | bytes 5500000 | tf_op jit(solution)/shard_map/pallas_call | solution.py:520
  44.9 0.8 %copy.16 = bf16[256,1024]{1,0:T(8,128)(2,1)} copy(bf16[256,1024]{1,0:T(8,128)(2,1)S(1)} %get-tuple-element.6) | data formatting | bytes 1048576
  45.7 0.8 %copy.17 = bf16[256,1024]{1,0:T(8,128)(2,1)} copy(bf16[256,1024]{1,0:T(8,128)(2,1)S(1)} %get-tuple-element.7) | data formatting | bytes 1048576
  46.5 0.6 %copy.18 = bf16[96,512]{1,0:T(8,128)(2,1)} copy(bf16[96,512]{1,0:T(8,128)(2,1)S(1)} %get-tuple-element.8) | data formatting | bytes 196608
Async XLA Ops:
  0.6 0.7 %copy-start.2 = (f32[128]{0:T(128)S(1)}, f32[128]{0:T(128)}, u32[]{:S(2)}) copy-start(f32[128]{0:T(128)} %param.15) | copy-start | bytes 1540
  0.6 0.7 %copy-start.3 = (s32[64]{0:T(128)S(1)}, s32[64]{0:T(128)}, u32[]{:S(2)}) copy-start(s32[64]{0:T(128)} %slot_hbm.1) | copy-start | bytes 772
  0.7 0.7 %copy-start.4 = (s32[64]{0:T(128)S(1)}, s32[64]{0:T(128)}, u32[]{:S(2)}) copy-start(s32[64]{0:T(128)} %tiles_hbm.1) | copy-start | bytes 772
  0.7 0.7 %copy-start = (s32[4,2]{0,1:T(2,128)S(1)}, s32[4,2]{0,1:T(2,128)}, u32[]{:S(2)}) copy-start(s32[4,2]{0,1:T(2,128)} %param.18) | copy-start | bytes 100
  0.7 0.7 %copy-start.1 = (f32[128]{0:T(128)S(1)}, f32[128]{0:T(128)}, u32[]{:S(2)}) copy-start(f32[128]{0:T(128)} %param.14) | copy-start | bytes 1540
